TPU v7x, 128 devices: a whole 4x4x4 slice. The times are simulated.
128 devices in a mesh: lon: 16 (over y, z_hi, core), lat: 8 (over z_lo, x).
Axes of the slice: x: 4, y: 4, z: 4 (z_hi: 2, z_lo: 2; z = z_hi * 2 + z_lo), core: 2. Of those that a mesh axis runs over, the one named last changes fastest.
Arguments:
- background: float32 [69, 128, 2048], P(None, 'lon', 'lat'), may hold values from -6 to 6
- encoder_weight: bfloat16 [128, 69], replicated, may hold values from -0.75 to 0.75
- convolution_weight: bfloat16 [4, 9, 128, 128], replicated, may hold values from -0.1875 to 0.1875
- decoder_weight: bfloat16 [69, 128], replicated, may hold values from -0.5 to 0.5
- dilations: int32 [4], replicated, may hold values from 1 to 4, as said below
- obs_values: float32 [69, 65536], P(None, ('lon', 'lat')), may hold values from -6 to 6
- obs_prec: float32 [65536], P(('lon', 'lat')), may hold values from 0.25 to 4
- obs_frac: float32 [2, 65536], P(None, ('lon', 'lat')), may hold values from 0 to 1
- obs_dest: int32 [65536, 1], P(('lon', 'lat')), may hold values from 0 to 127; in each aligned block of 512 rows (0 to 511, 512 to 1023, ...) at most 8 rows name the same one
- obs_cell: int32 [65536], P(('lon', 'lat')), may hold values from 0 to 1784
- obs_count: int32 [128], P(('lon', 'lat')), may hold values from 256 to 512, as said below
Outputs:
- analysis: float32 [69, 128, 2048], P(None, 'lon', 'lat')
- innovations: float32 [69, 65536], P(None, ('lon', 'lat'))
Inputs may be any that keep to these rules, and one draw needn't show every extreme that they name: `dilations`: every layer's dilation lies in 1 to 4, and some layer has dilation 4. `obs_dest`: devices are numbered 8 * lon index + lat index. Among the 512 rows of one device no owner is named more than 8 times, a bound that some block reaches. `obs_cell`: the code c places the lower stencil corner at local longitude c // 255 and local latitude c % (255) of the owner's block, so all four stencil cells lie in that block. `obs_count`: some device has all 512 rows live.
All inputs are finite; a program needn't handle non-finite values.
Results may differ from a plain program's by a relative error of at most 0.023.
Values may be sent and summed in bfloat16 or wider, within the bound.
No kernel may reach another device: no remote copies, remote signals or barrier semaphores. Data moves between devices by JAX's collectives and lax.ppermute only.
A program may use at most 128 MiB of HBM per device.

v0:
```python
import functools

import jax
import jax.numpy as jnp
from jax import lax
from jax.experimental import pallas as pl
from jax.experimental.pallas import tpu as pltpu
from jax.sharding import PartitionSpec as P

AXES = ("lon", "lat")
BF = jnp.bfloat16
F32 = jnp.float32
V = 72
OFF = 8
ROWS = 96
R = 16
STEP = 0.25
VMEM = 60 * 1024 * 1024


def snake(s, lat):
    return s if lat % 2 == 0 else 3 - s


def device(lon, lat):
    return 8 * lon + lat


def worker(y, p):
    lat, k = p // 4, p % 4
    return device(4 * y + snake(k, lat), lat)


LON_UP = [(worker(y, p), worker((y + 1) % 4, p)) for y in range(4) for p in range(32)]
LON_DOWN = [(b, a) for a, b in LON_UP]
LAT_UP = [(worker(y, p), worker(y, p + 1)) for y in range(4) for p in range(31)]
LAT_DOWN = [(b, a) for a, b in LAT_UP]
BAND_UP = [(device(n, l), device(n, l + 1)) for n in range(16) for l in range(7)]
BAND_DOWN = [(b, a) for a, b in BAND_UP]
GROUPS_32 = [[device(4 * y + s, l) for y in range(4) for l in range(8)] for s in range(4)]
GROUPS_4 = [[device(4 * y + s, l) for s in range(4)] for y in range(4) for l in range(8)]


def family(m):
    pairs = []
    for y in range(4):
        for s in range(4):
            to = y if m < 4 else (y + (1 if s >= 2 else -1)) % 4
            for l in range(8):
                pairs.append((device(4 * y + s, l), device(4 * to + (s + m) % 4, l)))
    return pairs


def nt(a, b):
    return lax.dot_general(a, b, (((1,), (1,)), ((), ())), preferred_element_type=F32)


def tn(a, b):
    return lax.dot_general(a, b, (((0,), (0,)), ((), ())), preferred_element_type=F32)


def nn(a, b):
    return jnp.dot(a, b, preferred_element_type=F32)


def compact_kernel(scal, pay0, pay1, pay2, pay3, comp, posx, count, total):
    pays = (pay0, pay1, pay2, pay3)
    k64 = scal[6].astype(F32)
    mine, own = [], []
    for part in range(4):
        ctrl = pays[part][...].astype(F32)[72:80]
        local = ctrl[7:8] - k64
        live = ctrl[0:1] > 0.0
        mine.append(jnp.where(live & (local >= -1.0) & (local <= 63.0), 1.0, 0.0))
        own.append(jnp.where(live & (local >= 0.0) & (local <= 63.0), 1.0, 0.0))
    mine = jnp.concatenate([m[:, 128 * c : 128 * c + 128] for m in mine for c in range(8)], axis=0)
    own = jnp.concatenate([m[:, 128 * c : 128 * c + 128] for m in own for c in range(8)], axis=0)
    row = lax.broadcasted_iota(jnp.int32, (128, 128), 0)
    col = lax.broadcasted_iota(jnp.int32, (128, 128), 1)
    before = nn(mine.astype(BF), jnp.where(row < col, 1.0, 0.0).astype(BF))
    sums = nn(mine.astype(BF), jnp.ones((128, 128), BF))
    row4 = lax.broadcasted_iota(jnp.int32, (32, 32), 0)
    col4 = lax.broadcasted_iota(jnp.int32, (32, 32), 1)
    offset = nn(jnp.where(col4 < row4, 1.0, 0.0).astype(BF), sums.astype(BF))
    place = before + offset
    owned = jnp.where(own > 0.0, place, -1.0)
    for m in range(4):
        posx[pl.ds(pl.multiple_of(8 * (scal[8 + m] - 2), 8), 8), :] = owned[8 * m : 8 * m + 8]
    total[...] = jnp.where(mine > 0.0, place, -1.0)
    number = jnp.sum(mine).astype(jnp.int32)
    count[0] = number
    comp[...] = jnp.zeros_like(comp)
    index = lax.broadcasted_iota(jnp.int32, (256, 128), 0).astype(F32)

    @pl.loop(0, (number + 255) // 256)
    def _(tile):
        ids = index + (tile * 256).astype(F32)
        out = jnp.zeros((80, 256), F32)
        for c in range(0, 32, 2):
            picks = jnp.concatenate(
                [jnp.where(ids == total[c + h : c + h + 1, :], 1.0, 0.0).astype(BF) for h in (0, 1)], axis=1
            )
            out = out + nt(pays[c // 8][:, 128 * (c % 8) : 128 * (c % 8) + 256], picks)
        comp[:, pl.ds(pl.multiple_of(tile * 256, 256), 256)] = out.astype(BF)


def expand_kernel(count, posx, found, out, total):
    index = lax.broadcasted_iota(jnp.int32, (256, 128), 0).astype(F32)
    total[...] = jnp.zeros_like(total)

    @pl.loop(0, (count[0] + 255) // 256)
    def _(tile):
        ids = index + (tile * 256).astype(F32)
        rows = found[:, pl.ds(pl.multiple_of(tile * 256, 256), 256)]
        for c in range(32):
            picks = jnp.where(ids == posx[c : c + 1, :], 1.0, 0.0).astype(BF)
            to = 128 * (8 * (c % 8 // 2) + 2 * (c // 8) + c % 2)
            total[:, to : to + 128] += nn(rows, picks)

    out[...] = total[...].astype(BF)


def convolve(act, weight, d, first, count, store):
    for dd in range(1, 5):
        blocks = 8 // dd
        step = 2 * blocks * dd

        @pl.when(d == dd)
        def _():
            @pl.loop(0, (count + step - 1) // step)
            def _(c):
                i = first + step * c
                x = act[pl.ds(i - dd, step + 2 * dd)].reshape(blocks + 1, 2, dd, 96, 384)
                m = blocks * dd * 96
                x = [x[p // 2 : p // 2 + blocks, p % 2].reshape(m, 384) for p in range(4)]
                y = nn(jnp.concatenate(x, axis=1), weight[...])
                y = jnp.stack([y[:, 128 * p : 128 * p + 128].reshape(blocks, dd, 96, 128) for p in (0, 1)], axis=1)
                store(pl.ds(i, step), y.reshape(step, 96, 128))


def iterate(second, *refs):
    scal, count = refs[0:2]
    chunks = refs[2:10]
    enc_t, enc_eye, dec_eye, dec_n, eye, wf, wb, comp = refs[10:18]
    refs = refs[18:]
    if second:
        tots, from_prev, from_next = refs[0:2], refs[2], refs[3]
        outs, found = refs[4:12], refs[12]
        refs = refs[13:]
    else:
        outs = refs[0:2]
        refs = refs[2:]
    st, h, act, slope, bk, fct, wobs, g, ga, shift = refs

    act[...] = jnp.zeros_like(act)

    for f in range(8):
        base = 8 * scal[8 + f]
        for r in range(8):
            st[base + r] = tn(chunks[f][r], eye[...])
    if second:
        for half in range(2):
            tot = tots[half]
            for c in range(2):
                rows = pl.ds(32 * half + 16 * c, 16)
                lanes = 1024 * half + 512 * c
                for sec in range(3):
                    add = tot[:, 1024 * sec + 512 * c : 1024 * sec + 512 * c + 512].astype(F32)
                    if sec == 0:
                        add = add + from_prev[:, lanes : lanes + 512].astype(F32)
                    if sec == 2:
                        add = add + from_next[:, lanes : lanes + 512].astype(F32)
                    add = tn(add.astype(BF), eye[...]).reshape(16, 32, 128)
                    st[rows, 16 + 32 * sec : 48 + 32 * sec, :] -= STEP * add
                    if half + c == 1:
                        ga[pl.ds(16 * c_own(half, c), 16), 32 * sec : 32 * sec + 32, :] = 0.75 * add
            low = tn(from_prev[:, 2048 + 128 * half : 2176 + 128 * half], eye[...])
            high = tn(from_next[:, 2048 + 128 * half : 2176 + 128 * half], eye[...])
            for i in range(32):
                st[32 * half + i, 15:16, :] -= STEP * low[32 + i : 33 + i]
                st[32 * half + i, 112:113, :] -= STEP * high[i : i + 1]

    @pl.loop(0, 8)
    def _(c):
        x = st[pl.ds(8 * c, 8)].reshape(1024, 128).astype(BF)
        h[pl.ds(8 * c + OFF, 8)] = nn(x, enc_t[...]).reshape(8, 128, 128)

    e = lax.broadcasted_iota(jnp.int32, (112, 128), 0) + 8
    mask = jnp.where((e >= scal[4]) & (e < scal[5]), 1.0, 0.0)

    @pl.loop(0, 4)
    def _(l):
        d, reach = scal[l], scal[16 + l]
        first = 16 - reach - d + OFF

        @pl.loop(0, 16 + reach + d)
        def _(q):
            for u in range(2):
                i = first + 2 * q + u
                t = jnp.tanh(h[i, 8:120, :])
                slope[l, i] = ((1.0 - t * t) * mask)[8:104].astype(BF)
                t = t * mask
                shift[u] = t
                act[i, :, 0:128] = shift[u, pl.ds(8 - d, 96), :].astype(BF)
                act[i, :, 128:256] = t[8:104].astype(BF)
                act[i, :, 256:384] = shift[u, pl.ds(8 + d, 96), :].astype(BF)

        for u in range(R):
            slope[l, 48 + reach + d + OFF + u] = jnp.zeros((96, 128), BF)

        def store(rows, y):
            h[rows, 16:112, :] += y

        convolve(act, wf.at[l], d, 16 - reach + OFF, 32 + 2 * reach, store)

    for c in range(4):
        a = h[16 + OFF + 8 * c : 24 + OFF + 8 * c, 16:112, :].reshape(768, 128).astype(BF)
        b = st[16 + 8 * c : 24 + 8 * c, 16:112, :].reshape(768, 128).astype(BF)
        fct[:, 768 * c : 768 * c + 768] = nt(dec_eye[...], jnp.concatenate([a, b], axis=1)).astype(BF)

    g[...] = jnp.zeros_like(g)
    k64 = scal[6].astype(F32)
    lon_of = lax.broadcasted_iota(jnp.int32, (32, 256), 0).astype(F32)
    lat_of = lax.broadcasted_iota(jnp.int32, (96, 256), 0).astype(F32) - 16.0

    @pl.loop(0, (count[0] + 255) // 256)
    def _(tile):
        lanes = pl.ds(pl.multiple_of(tile * 256, 256), 256)
        pay = comp[:, lanes].astype(F32)
        prec = pay[72:73] + pay[73:74]
        fu = pay[74:75] + pay[75:76]
        fv = pay[76:77] + pay[77:78]
        li, lj = pay[78:79], pay[79:80] - k64
        wa = jnp.where(lon_of == li, 1.0 - fu, 0.0) + jnp.where(lon_of == li + 1.0, fu, 0.0)
        wl = (jnp.where(lat_of == lj, 1.0 - fv, 0.0) + jnp.where(lat_of == lj + 1.0, fv, 0.0)).astype(BF)
        wa = wa.astype(BF)
        for i in range(32):
            wobs[96 * i : 96 * i + 96, :] = wa[i : i + 1] * wl
        eq = nn(fct[...], wobs[...])
        if second:
            found[:, lanes] = eq.astype(BF)
        wt = (prec * (eq - pay[0:72])).astype(BF)
        wt = jnp.concatenate([wt, jnp.zeros((56, 256), BF)], axis=0)
        for c in range(4):
            g[pl.ds(8 * c, 8)] += nt(wobs[768 * c : 768 * c + 768, :], wt).reshape(8, 96, 128)

    g[:, 0:16, :] = jnp.zeros((32, 16, 128), F32)
    g[:, 80:96, :] = jnp.zeros((32, 16, 128), F32)

    bk[...] = jnp.zeros_like(bk)
    act[0:24] = jnp.zeros((24, 96, 384), BF)
    act[56:96] = jnp.zeros((40, 96, 384), BF)
    for c in range(4):
        x = g[8 * c : 8 * c + 8].reshape(768, 128).astype(BF)
        bk[16 + OFF + 8 * c : 24 + OFF + 8 * c, 8:104, :] = nn(x, dec_n[...]).reshape(8, 96, 128)

    @pl.loop(0, 4)
    def _(back):
        l = 3 - back
        d, reach = scal[l], scal[16 + l]
        first = 16 - reach + OFF

        @pl.loop(0, 16 + reach)
        def _(q):
            for u in range(2):
                i = first + 2 * q + u
                act[i, :, 0:128] = bk[i, pl.ds(8 - d, 96), :].astype(BF)
                act[i, :, 128:256] = bk[i, 8:104, :].astype(BF)
                act[i, :, 256:384] = bk[i, pl.ds(8 + d, 96), :].astype(BF)

        def store(rows, y):
            bk[rows, 8:104, :] += slope[l, rows].astype(F32) * y

        convolve(act, wb.at[l], d, first - d, 32 + 2 * (reach + d), store)

    if second:
        ga[:, 0:16, :] = jnp.zeros((32, 16, 128), F32)
        ga[:, 80:96, :] = jnp.zeros((32, 16, 128), F32)
        for f in range(8):
            base = 8 * scal[8 + f]
            inside = (base >= 16) & (base < 48)
            grow = jnp.where(inside, base - 16, 0)
            keep = jnp.where(inside, 1.0, 0.0)
            for r in range(8):
                x = bk[base + r + OFF, 8:104, :].astype(BF)
                y = (keep * (g[grow + r] + ga[grow + r])).astype(BF)
                x = jnp.concatenate([x, y], axis=1)
                edge = jnp.zeros((16, 256), BF)
                x = jnp.concatenate([edge, x, edge], axis=0)
                outs[f][r] = (-STEP * nt(enc_eye[...], x)).astype(BF)
    else:
        for half in range(2):
            for c in range(2):
                lo = 32 * half + 16 * c
                for sec in range(3):
                    x = bk[lo + OFF : lo + OFF + 16, 32 * sec + 8 : 32 * sec + 40, :].reshape(512, 128).astype(BF)
                    if half + c == 1:
                        y = g[lo - 16 : lo, 32 * sec : 32 * sec + 32, :].reshape(512, 128).astype(BF)
                        val = nt(enc_eye[...], jnp.concatenate([x, y], axis=1))
                    else:
                        val = nt(enc_eye[:, 0:128], x)
                    outs[half][:, 1024 * sec + 512 * c : 1024 * sec + 512 * c + 512] = val.astype(BF)
            rows = []
            for col in (32, 63):
                for i in range(32):
                    x = bk[32 * half + i + OFF, col + 8 : col + 9, :]
                    here = 32 * half + i - 16
                    if 0 <= here < 32:
                        y = g[here, col : col + 1, :]
                    else:
                        y = jnp.zeros((1, 128), F32)
                    rows.append(jnp.concatenate([x, y], axis=1))
            rows.append(jnp.zeros((64, 256), F32))
            x = jnp.concatenate(rows, axis=0).astype(BF)
            outs[half][:, 3072:3200] = nt(enc_eye[...], x).astype(BF)


def c_own(half, c):
    return 0 if (half, c) == (0, 1) else 1


def iteration(second, scal, count, *arrays):
    smem = pl.BlockSpec(memory_space=pltpu.SMEM)
    vmem = pl.BlockSpec(memory_space=pltpu.VMEM)
    if second:
        shapes = [jax.ShapeDtypeStruct((8, V, 128), BF)] * 8 + [jax.ShapeDtypeStruct((V, 4096), BF)]
    else:
        shapes = [jax.ShapeDtypeStruct((V, 3200), BF)] * 2
    return pl.pallas_call(
        functools.partial(iterate, second),
        out_shape=shapes,
        in_specs=[smem, smem] + [vmem] * len(arrays),
        out_specs=[vmem] * len(shapes),
        scratch_shapes=[
            pltpu.VMEM((64, 128, 128), F32),
            pltpu.VMEM((ROWS, 128, 128), F32),
            pltpu.VMEM((ROWS, 96, 384), BF),
            pltpu.VMEM((4, ROWS, 96, 128), BF),
            pltpu.VMEM((ROWS, 112, 128), F32),
            pltpu.VMEM((V, 3072), BF),
            pltpu.VMEM((3072, 256), BF),
            pltpu.VMEM((32, 96, 128), F32),
            pltpu.VMEM((32, 96, 128), F32),
            pltpu.VMEM((2, 112, 128), F32),
        ],
        compiler_params=pltpu.CompilerParams(vmem_limit_bytes=VMEM),
        cost_estimate=pl.CostEstimate(flops=10**10, bytes_accessed=6 * 10**6, transcendentals=3 * 10**6),
        name="second_iteration" if second else "first_iteration",
    )(scal, count, *arrays)


def paired(taps):
    none = jnp.zeros((taps.shape[0], 384, 128), BF)
    low, mid, top = taps[:, 0], taps[:, 1], taps[:, 2]
    first = jnp.concatenate([low, mid, top, none], axis=1)
    later = jnp.concatenate([none, low, mid, top], axis=1)
    return jnp.concatenate([first, later], axis=2)


def make_weights(encoder_weight, convolution_weight, decoder_weight):
    eye = jnp.eye(V, 128, dtype=BF)
    enc_v = jnp.pad(encoder_weight.T, ((0, 128 - 69), (0, 0)))
    dec_v = jnp.pad(decoder_weight, ((0, 128 - 69), (0, 0)))
    ahead = convolution_weight.transpose(0, 1, 3, 2).reshape(4, 3, 384, 128)
    back = convolution_weight[:, ::-1].reshape(4, 3, 384, 128)
    return (
        enc_v,
        jnp.concatenate([enc_v[0:V], eye], axis=1),
        jnp.concatenate([dec_v[0:V], eye], axis=1),
        dec_v,
        eye,
        paired(ahead),
        paired(back),
    )


def on_device(
    background,
    encoder_weight,
    convolution_weight,
    decoder_weight,
    dilations,
    obs_values,
    obs_prec,
    obs_frac,
    obs_dest,
    obs_cell,
    obs_count,
):
    smem = pl.BlockSpec(memory_space=pltpu.SMEM)
    vmem = pl.BlockSpec(memory_space=pltpu.VMEM)
    lon, lat = lax.axis_index("lon"), lax.axis_index("lat")
    sub = lon % 4
    flip = lat % 2 == 1

    def block_of(s):
        return jnp.where(flip, 3 - s, s)

    k = block_of(sub)
    top = 256 * lat + 64 * k
    came = [(sub - m) % 4 for m in range(4)]
    tables = [c + 2 for c in came] + [jnp.where(c >= 2, c - 2, c + 6) for c in came]
    d = dilations
    scal = jnp.stack(
        [d[0], d[1], d[2], d[3], 32 - top, 2048 + 32 - top, 64 * k, jnp.int32(0)]
        + tables
        + [d[1] + d[2] + d[3], d[2] + d[3], d[3], jnp.int32(0)]
    ).astype(jnp.int32)

    rows = obs_dest.shape[0]
    owner = obs_dest[:, 0]
    group = (owner // 32) * 8 + owner % 8
    member = (group[:, None] == jnp.arange(32, dtype=jnp.int32)[None, :]).astype(BF)
    order = jnp.arange(rows, dtype=jnp.int32)
    earlier = (order[None, :] < order[:, None]).astype(BF)
    rank = jnp.sum(nn(earlier, member) * member.astype(F32), axis=1).astype(jnp.int32)
    slots = group * 32 + rank
    alive = (jnp.arange(rows, dtype=jnp.int32) < obs_count[0]).astype(F32)
    prec = alive * obs_prec
    wide = jnp.stack([prec, obs_frac[0], obs_frac[1]])
    high = wide.astype(BF)
    low = (wide - high.astype(F32)).astype(BF)
    li = 8 * ((owner // 8) % 4) + obs_cell // 255
    lj = obs_cell % 255
    payload = jnp.concatenate(
        [
            obs_values.astype(BF),
            jnp.zeros((3, rows), BF),
            jnp.stack([high[0], low[0], high[1], low[1], high[2], low[2], li.astype(BF), lj.astype(BF)]),
        ]
    )
    pick = (slots[:, None] == jnp.arange(1024, dtype=jnp.int32)[None, :]).astype(BF)
    packed = jnp.einsum("vr,rs->vs", payload, pick, preferred_element_type=F32).astype(BF)
    arrived = lax.all_to_all(packed, AXES, split_axis=1, concat_axis=1, tiled=True, axis_index_groups=GROUPS_32)
    others = [
        lax.ppermute(arrived, AXES, [(g[s], g[(s + m) % 4]) for g in GROUPS_4 for s in range(4)]) for m in range(1, 4)
    ]
    comp, posx, count = pl.pallas_call(
        compact_kernel,
        out_shape=[
            jax.ShapeDtypeStruct((80, 4096), BF),
            jax.ShapeDtypeStruct((32, 128), F32),
            jax.ShapeDtypeStruct((1,), jnp.int32),
        ],
        in_specs=[smem] + [vmem] * 4,
        out_specs=[vmem, vmem, smem],
        scratch_shapes=[pltpu.VMEM((32, 128), F32)],
        name="compact",
    )(scal, arrived, *others)

    cells = jnp.pad(background.astype(BF).transpose(1, 0, 2), ((0, 0), (0, V - 69), (0, 0)))
    before = lax.ppermute(cells[:, :, 224:256], AXES, BAND_UP)
    after = lax.ppermute(cells[:, :, 0:32], AXES, BAND_DOWN)
    band = jnp.concatenate([before, cells, after], axis=2)
    parts = jnp.stack([band[:, :, 64 * b : 64 * b + 128] for b in range(4)])
    sends = [lax.dynamic_index_in_dim(parts, block_of((sub + m) % 4), 0, keepdims=False) for m in range(4)]
    chunks = [sends[0]] + [lax.ppermute(sends[m % 4], AXES, family(m)) for m in range(1, 8)]

    weights = make_weights(encoder_weight, convolution_weight, decoder_weight)

    left, right = iteration(False, scal, count, *chunks, *weights, comp)
    left_in = lax.ppermute(right, AXES, LON_UP)
    right_in = lax.ppermute(left, AXES, LON_DOWN)
    left = (left.astype(F32) + left_in.astype(F32)).astype(BF)
    right = (right.astype(F32) + right_in.astype(F32)).astype(BF)
    extra = [left[:, 3072:3200], right[:, 3072:3200]]
    from_next = lax.ppermute(jnp.concatenate([left[:, 0:1024], right[:, 0:1024]] + extra, axis=1), AXES, LAT_DOWN)
    from_prev = lax.ppermute(jnp.concatenate([left[:, 2048:3072], right[:, 2048:3072]] + extra, axis=1), AXES, LAT_UP)
    *moves, found = iteration(True, scal, count, *chunks, *weights, comp, left, right, from_prev, from_next)

    spread = pl.pallas_call(
        expand_kernel,
        out_shape=jax.ShapeDtypeStruct((V, 4096), BF),
        in_specs=[smem, vmem, vmem],
        out_specs=vmem,
        scratch_shapes=[pltpu.VMEM((V, 4096), F32)],
        name="expand",
    )(count, posx, found)
    *moves, spread = lax.optimization_barrier((*moves, spread))
    spread = lax.all_to_all(spread, AXES, split_axis=1, concat_axis=1, tiled=True)
    spread = [spread[:, 256 * c : 256 * c + 256] for c in range(16)]
    spread = jnp.concatenate(
        [spread[4 * y] + spread[4 * y + 1] + spread[4 * y + 2] + spread[4 * y + 3] for y in range(4)], axis=1
    )
    equivalent = jnp.einsum("vs,rs->vr", spread[0:69], pick, preferred_element_type=F32)
    innovation = alive[None, :] * (equivalent - obs_values)

    back = [moves[0]] + [lax.ppermute(moves[m], AXES, [(b, a) for a, b in family(m)]) for m in range(1, 8)]
    total = jnp.zeros((8, V, 320), F32)
    summed = jnp.stack([back[m].astype(F32) + back[m + 4].astype(F32) for m in range(4)])
    for b in range(4):
        m = (jnp.where(flip, 3 - b, b) - sub) % 4
        block = lax.dynamic_index_in_dim(summed, m, 0, keepdims=False)
        total = total + jnp.pad(block, ((0, 0), (0, 0), (64 * b, 192 - 64 * b)))
    edge_up = lax.ppermute(total[:, :, 288:320].astype(BF), AXES, BAND_UP)
    edge_down = lax.ppermute(total[:, :, 0:32].astype(BF), AXES, BAND_DOWN)
    total = total[:, :, 32:288]
    total = total + jnp.pad(edge_up.astype(F32), ((0, 0), (0, 0), (0, 224)))
    total = total + jnp.pad(edge_down.astype(F32), ((0, 0), (0, 0), (224, 0)))
    analysis = background + total[:, 0:69, :].transpose(1, 0, 2)
    return (analysis, innovation)


def solution(mesh):
    placed = (
        P(None, "lon", "lat"),
        P(),
        P(),
        P(),
        P(),
        P(None, ("lon", "lat")),
        P(("lon", "lat")),
        P(None, ("lon", "lat")),
        P(("lon", "lat"), None),
        P(("lon", "lat")),
        P(("lon", "lat")),
    )
    return jax.shard_map(
        on_device,
        mesh=mesh,
        in_specs=placed,
        out_specs=(P(None, "lon", "lat"), P(None, ("lon", "lat"))),
        check_vma=False,
    )
```

profile of v0, /device:TPU:6, one launch (start us, length us, event | category | flops | bytes accessed | tf_op | source)
XLA Modules:
  0.0 242.1 jit_solution(1209496745034140328)
XLA Ops:
  0.6 1.2 convert_bitcast_fusion
  2.5 0.8 pad_slice_fusion.3
  3.3 3.7 %collective-permute-start.3 = (bf16[8,72,32]{2,0,1:T(8,128)(2,1)}, bf16[8,72,32]{2,0,1:T(8,128)(2,1)}, u32[]{:S(2)}, u32[]{:S(2)}) collective-permute-start(bf16[8,72,32]{2,0,1:T(8,128)(2,1)} %get-tuple-element.80), channel_id=1, source_target_pairs={{0,1},{1,2},{2,3},{3,4},{4,5},{5,6},{6,7},{8,9},{9,10},{10,11},{11... | collective-permute-start | bytes 110600 | tf_op jit(solution)/shard_map/ppermute | solution.py:452
  7.0 2.1 collective-permute-start.4
  12.6 0.7 fusion.29
  13.3 0.9 convert_element_type.124
  15.9 0.8 copy.17
  16.8 9.4 %all-to-all-start = ((bf16[80,32,32]{0,2,1:T(8,128)(2,1)}), bf16[80,32,32]{0,2,1:T(8,128)(2,1)}, u32[]{:S(2)}, u32[]{:S(2)}) async-start(bf16[80,32,32]{0,2,1:T(8,128)(2,1)} %bitcast.22), calls=%async_computation | async-start | bytes 524288 | tf_op jit(solution)/shard_map/all_to_all | solution.py:434
  26.2 0.7 copy.26
  27.3 3.3 %fusion.1 = (bf16[4,1536,256]{2,1,0:T(8,128)(2,1)}, bf16[4,1536,256]{2,1,0:T(8,128)(2,1)}) fusion(bf16[4,384,128]{2,1,0:T(8,128)(2,1)S(1)} %broadcast.99, bf16[4,384,128]{2,1,0:T(8,128)(2,1)S(1)} %get-tuple-element.58, bf16[4,384,128]{2,1,0:T(8,128)(2,1)S(1)} %get-tuple-element.57, bf16[4,384,128]{2,1,0:T(8,128)(2,1)S(1)} %get-tuple-element.56, ...), kind=kLoop, calls=%fused_computation.5 | loop fusion | flops 47185920 | bytes 9043968 | tf_op jit(solution)/shard_map/concatenate | solution.py:357
  30.9 1.2 fusion.19
  32.3 5.8 %collective-permute-start.10 = (bf16[8,72,128]{2,1,0:T(8,128)(2,1)S(1)}, bf16[8,72,128]{2,1,0:T(8,128)(2,1)S(1)}, u32[]{:S(2)}, u32[]{:S(2)}) collective-permute-start(bf16[8,72,128]{2,1,0:T(8,128)(2,1)S(1)} %bitcast.106), channel_id=1, source_target_pairs={{0,112},{1,113},{2,114},{3,115},{4,116},{5,117},{6,118},{7,119},{8... | collective-permute-start | bytes 442376 | tf_op jit(solution)/shard_map/ppermute | solution.py:457
  38.2 1.1 copy.21.pay0
  39.3 1.0 collective-permute-start
  40.3 2.9 %collective-permute-start.2 = (bf16[80,1024]{1,0:T(8,128)(2,1)S(1)}, bf16[80,1024]{1,0:T(8,128)(2,1)S(1)}, u32[]{:S(2)}, u32[]{:S(2)}) collective-permute-start(bf16[80,1024]{1,0:T(8,128)(2,1)S(1)} %copy.21.pay0), channel_id=1, source_target_pairs={{0,24},{8,0},{16,8},{24,16},{1,25},{9,1},{17,9},{25,17},{2,26},{10... | collective-permute-start | bytes 491528 | tf_op jit(solution)/shard_map/ppermute | solution.py:436
  43.4 2.7 %collective-permute-start.6 = (bf16[8,72,128]{2,1,0:T(8,128)(2,1)S(1)}, bf16[8,72,128]{2,1,0:T(8,128)(2,1)S(1)}, u32[]{:S(2)}, u32[]{:S(2)}) collective-permute-start(bf16[8,72,128]{2,1,0:T(8,128)(2,1)S(1)} %bitcast.107), channel_id=1, source_target_pairs={{0,16},{1,17},{2,18},{3,19},{4,20},{5,21},{6,22},{7,23},{8,24},{9,... | collective-permute-start | bytes 442376 | tf_op jit(solution)/shard_map/ppermute | solution.py:457
  46.2 2.0 collective-permute-done.pay1
  48.1 0.8 collective-permute-done.1.pay2
  49.0 3.9 %collective-permute-start.9 = (bf16[8,72,128]{2,1,0:T(8,128)(2,1)S(1)}, bf16[8,72,128]{2,1,0:T(8,128)(2,1)S(1)}, u32[]{:S(2)}, u32[]{:S(2)}) collective-permute-start(bf16[8,72,128]{2,1,0:T(8,128)(2,1)S(1)} %bitcast.111), channel_id=1, source_target_pairs={{0,104},{1,105},{2,106},{3,107},{4,108},{5,109},{6,110},{7,111},{8... | collective-permute-start | bytes 442376 | tf_op jit(solution)/shard_map/ppermute | solution.py:457
  58.6 1.2 stack.98.scal.refs_0_
  60.5 3.9 %compact.1 = (bf16[80,4096]{1,0:T(8,128)(2,1)}, f32[32,128]{1,0:T(8,128)}, s32[1]{0:T(128)}) custom-call(s32[20]{0:T(128)} %stack.98.scal.refs_0_, bf16[80,1024]{1,0:T(8,128)(2,1)} %copy-done.6, bf16[80,1024]{1,0:T(8,128)(2,1)} %copy-done.7, bf16[80,1024]{1,0:T(8,128)(2,1)} %copy-done.8, bf16[80,1024]{1,0:T(8,128)(2,1)} %copy-done.9), custom_call_target="tpu_custom_call" | custom-call | tf_op jit(solution)/shard_map/compact/pallas_call | solution.py:438
  65.3 40.4 %first_iteration.1 = (bf16[72,3200]{1,0:T(8,128)(2,1)}, bf16[72,3200]{1,0:T(8,128)(2,1)}) custom-call(s32[20]{0:T(128)} %stack.98.scal.refs_0_, s32[1]{0:T(128)} %get-tuple-element.25.refs_1_.count, bf16[8,72,128]{2,1,0:T(8,128)(2,1)} %bitcast.104, bf16[8,72,128]{2,1,0:T(8,128)(2,1)} %copy-done.23, bf16[8,72,128]{2,1,0:T(8,128)(2,1)} %copy-done.21, ...), custom_call_target="tpu_custom_call" | custom-call | flops 10000000000 | bytes 6000000 | tf_op jit(solution)/shard_map/first_iteration/pallas_call | solution.py:329
  105.7 2.0 collective-permute-start.12
  107.7 10.7 %collective-permute-done.13 = bf16[72,3200]{1,0:T(8,128)(2,1)S(1)} collective-permute-done((bf16[72,3200]{1,0:T(8,128)(2,1)}, bf16[72,3200]{1,0:T(8,128)(2,1)S(1)}, u32[]{:S(2)}, u32[]{:S(2)}) %collective-permute-start.13) | collective-permute-done | bytes 460832 | tf_op jit(solution)/shard_map/ppermute | solution.py:463
  118.4 1.1 add_convert_fusion.refs_19_
  119.7 1.2 add_convert_fusion.1.refs_18_
  121.0 2.9 %collective-permute-start.14 = (bf16[72,2304]{1,0:T(8,128)(2,1)S(1)}, bf16[72,2304]{1,0:T(8,128)(2,1)S(1)}, u32[]{:S(2)}, u32[]{:S(2)}) collective-permute-start(bf16[72,2304]{1,0:T(8,128)(2,1)S(1)} %get-tuple-element.85), channel_id=1, source_target_pairs={{0,8},{8,16},{16,24},{24,25},{25,17},{17,9},{9,1},{1,2},{2,10},{10... | collective-permute-start | bytes 995336 | tf_op jit(solution)/shard_map/ppermute | solution.py:468
  123.8 1.9 collective-permute-start.15
  125.8 2.7 %collective-permute-done.14.refs_20_ = bf16[72,2304]{1,0:T(8,128)(2,1)S(1)} collective-permute-done((bf16[72,2304]{1,0:T(8,128)(2,1)S(1)}, bf16[72,2304]{1,0:T(8,128)(2,1)S(1)}, u32[]{:S(2)}, u32[]{:S(2)}) %collective-permute-start.14) | collective-permute-done | bytes 331808 | tf_op jit(solution)/shard_map/ppermute | solution.py:468
  128.5 6.6 %collective-permute-done.15.refs_21_ = bf16[72,2304]{1,0:T(8,128)(2,1)S(1)} collective-permute-done((bf16[72,2304]{1,0:T(8,128)(2,1)S(1)}, bf16[72,2304]{1,0:T(8,128)(2,1)S(1)}, u32[]{:S(2)}, u32[]{:S(2)}) %collective-permute-start.15) | collective-permute-done | bytes 331808 | tf_op jit(solution)/shard_map/ppermute | solution.py:467
  135.8 42.1 %second_iteration.1 = (bf16[8,72,128]{2,1,0:T(8,128)(2,1)}, bf16[8,72,128]{2,1,0:T(8,128)(2,1)}, bf16[8,72,128]{2,1,0:T(8,128)(2,1)}, bf16[8,72,128]{2,1,0:T(8,1...) custom-call(s32[20]{0:T(128)} %stack.98.scal.refs_0_, ...), custom_call_target="tpu_custom_call" | custom-call | flops 10000000000 | bytes 6000000 | tf_op jit(solution)/shard_map/second_iteration/pallas_call | solution.py:329
  178.0 3.7 %expand.1 = bf16[72,4096]{1,0:T(8,128)(2,1)} custom-call(s32[1]{0:T(128)} %get-tuple-element.25.refs_1_.count, f32[32,128]{1,0:T(8,128)} %get-tuple-element.37.posx, bf16[72,4096]{1,0:T(8,128)(2,1)} %get-tuple-element.38.found), custom_call_target="tpu_custom_call" | custom-call | tf_op jit(solution)/shard_map/expand/pallas_call | solution.py:471
  181.7 1.6 collective-permute-start.16
  183.3 2.2 copy.34
  185.5 12.0 %all-to-all-start.1 = ((bf16[72,128,32]{0,2,1:T(8,128)(2,1)}), bf16[72,128,32]{0,2,1:T(8,128)(2,1)S(1)}, u32[]{:S(2)}, u32[]{:S(2)}) async-start(bf16[72,128,32]{0,2,1:T(8,128)(2,1)} %bitcast.53), calls=%async_computation.1 | async-start | bytes 2097152 | tf_op jit(solution)/shard_map/all_to_all | solution.py:480
  197.5 3.2 %collective-permute-start.17 = (bf16[8,72,128]{2,1,0:T(8,128)(2,1)S(1)}, bf16[8,72,128]{2,1,0:T(8,128)(2,1)S(1)}, u32[]{:S(2)}, u32[]{:S(2)}) collective-permute-start(bf16[8,72,128]{2,1,0:T(8,128)(2,1)S(1)} %copy-done.31), channel_id=1, source_target_pairs={{8,0},{9,1},{10,2},{11,3},{12,4},{13,5},{14,6},{15,7},{16,8},{17,9... | collective-permute-start | bytes 442376 | tf_op jit(solution)/shard_map/ppermute | solution.py:488
  200.7 2.7 %collective-permute-start.18 = (bf16[8,72,128]{2,1,0:T(8,128)(2,1)S(1)}, bf16[8,72,128]{2,1,0:T(8,128)(2,1)S(1)}, u32[]{:S(2)}, u32[]{:S(2)}) collective-permute-start(bf16[8,72,128]{2,1,0:T(8,128)(2,1)S(1)} %copy-done.30), channel_id=1, source_target_pairs={{104,0},{105,1},{106,2},{107,3},{108,4},{109,5},{110,6},{111,7},{1... | collective-permute-start | bytes 442376 | tf_op jit(solution)/shard_map/ppermute | solution.py:488
  203.4 3.8 %collective-permute-start.20 = (bf16[8,72,128]{2,1,0:T(8,128)(2,1)S(1)}, bf16[8,72,128]{2,1,0:T(8,128)(2,1)S(1)}, u32[]{:S(2)}, u32[]{:S(2)}) collective-permute-start(bf16[8,72,128]{2,1,0:T(8,128)(2,1)S(1)} %copy-done.28), channel_id=1, source_target_pairs={{112,0},{113,1},{114,2},{115,3},{116,4},{117,5},{118,6},{119,7},{1... | collective-permute-start | bytes 442376 | tf_op jit(solution)/shard_map/ppermute | solution.py:488
  207.2 10.0 %collective-permute-done.17 = bf16[8,72,128]{2,1,0:T(8,128)(2,1)S(1)} collective-permute-done((bf16[8,72,128]{2,1,0:T(8,128)(2,1)S(1)}, bf16[8,72,128]{2,1,0:T(8,128)(2,1)S(1)}, u32[]{:S(2)}, u32[]{:S(2)}) %collective-permute-start.17) | collective-permute-done | bytes 147488 | tf_op jit(solution)/shard_map/ppermute | solution.py:488
  217.2 5.0 %collective-permute-start.22 = (bf16[8,72,128]{2,1,0:T(8,128)(2,1)S(1)}, bf16[8,72,128]{2,1,0:T(8,128)(2,1)S(1)}, u32[]{:S(2)}, u32[]{:S(2)}) collective-permute-start(bf16[8,72,128]{2,1,0:T(8,128)(2,1)S(1)} %copy-done.26), channel_id=1, source_target_pairs={{120,0},{121,1},{122,2},{123,3},{124,4},{125,5},{126,6},{127,7},{9... | collective-permute-start | bytes 442376 | tf_op jit(solution)/shard_map/ppermute | solution.py:488
  222.3 1.7 collective-permute-done.19
  224.0 2.2 collective-permute-done.21
  226.9 3.4 %collective-permute-start.23 = (bf16[8,72,32]{2,1,0:T(8,128)(2,1)S(1)}, bf16[8,72,32]{2,1,0:T(8,128)(2,1)S(1)}, u32[]{:S(2)}, u32[]{:S(2)}) collective-permute-start(bf16[8,72,32]{2,1,0:T(8,128)(2,1)S(1)} %get-tuple-element.74), channel_id=1, source_target_pairs={{0,1},{1,2},{2,3},{3,4},{4,5},{5,6},{6,7},{8,9},{9,10},{10,11},{11... | collective-permute-start | bytes 110600 | tf_op jit(solution)/shard_map/ppermute | solution.py:495
  230.4 2.4 %collective-permute-start.24 = (bf16[8,72,32]{2,1,0:T(8,128)(2,1)S(1)}, bf16[8,72,32]{2,1,0:T(8,128)(2,1)S(1)}, u32[]{:S(2)}, u32[]{:S(2)}) collective-permute-start(bf16[8,72,32]{2,1,0:T(8,128)(2,1)S(1)} %get-tuple-element.75), channel_id=1, source_target_pairs={{1,0},{2,1},{3,2},{4,3},{5,4},{6,5},{7,6},{9,8},{10,9},{11,10},{12... | collective-permute-start | bytes 110600 | tf_op jit(solution)/shard_map/ppermute | solution.py:496
  233.0 1.8 collective-permute-done.23
  234.8 4.7 %collective-permute-done.24 = bf16[8,72,32]{2,1,0:T(8,128)(2,1)S(1)} collective-permute-done((bf16[8,72,32]{2,1,0:T(8,128)(2,1)S(1)}, bf16[8,72,32]{2,1,0:T(8,128)(2,1)S(1)}, u32[]{:S(2)}, u32[]{:S(2)}) %collective-permute-start.24) | collective-permute-done | bytes 36896 | tf_op jit(solution)/shard_map/ppermute | solution.py:496
  239.8 1.0 copy.35
  240.8 1.3 fusion.10
  (136 shorter events, 12.1 us)
Async XLA Ops:
  0.6 25.5 %copy-start = (bf16[4,9,128,128]{3,2,1,0:T(8,128)(2,1)S(1)}, bf16[4,9,128,128]{3,2,1,0:T(8,128)(2,1)}, u32[]{:S(2)}) copy-start(bf16[4,9,128,128]{3,2,1,0:T(8,128)(2,1)} %param.13) | copy-start | bytes 3538948
  3.3 27.6 %collective-permute-start.3 = (bf16[8,72,32]{2,0,1:T(8,128)(2,1)}, bf16[8,72,32]{2,0,1:T(8,128)(2,1)}, u32[]{:S(2)}, u32[]{:S(2)}) collective-permute-start(bf16[8,72,32]{2,0,1:T(8,128)(2,1)} %get-tuple-element.80), channel_id=1, source_target_pairs={{0,1},{1,2},{2,3},{3,4},{4,5},{5,6},{6,7},{8,9},{9,10},{10,11},{11... | collective-permute-start | bytes 110600 | tf_op jit(solution)/shard_map/ppermute | solution.py:452
  7.0 23.9 %collective-permute-start.4 = (bf16[8,72,32]{2,0,1:T(8,128)(2,1)}, bf16[8,72,32]{2,0,1:T(8,128)(2,1)}, u32[]{:S(2)}, u32[]{:S(2)}) collective-permute-start(bf16[8,72,32]{2,0,1:T(8,128)(2,1)} %get-tuple-element.81), channel_id=1, source_target_pairs={{1,0},{2,1},{3,2},{4,3},{5,4},{6,5},{7,6},{9,8},{10,9},{11,10},{12... | collective-permute-start | bytes 110600 | tf_op jit(solution)/shard_map/ppermute | solution.py:453
  16.8 21.5 %all-to-all-start = ((bf16[80,32,32]{0,2,1:T(8,128)(2,1)}), bf16[80,32,32]{0,2,1:T(8,128)(2,1)}, u32[]{:S(2)}, u32[]{:S(2)}) async-start(bf16[80,32,32]{0,2,1:T(8,128)(2,1)} %bitcast.22), calls=%async_computation | async-start | bytes 524288 | tf_op jit(solution)/shard_map/all_to_all | solution.py:434
  30.6 12.7 %copy-start.13 = (bf16[128,69]{0,1:T(8,128)(2,1)S(1)}, bf16[128,69]{0,1:T(8,128)(2,1)}, u32[]{:S(2)}) copy-start(bf16[128,69]{0,1:T(8,128)(2,1)} %param.12) | copy-start | bytes 52996
  30.6 12.7 %copy-start.14 = (bf16[69,128]{1,0:T(8,128)(2,1)S(1)}, bf16[69,128]{1,0:T(8,128)(2,1)}, u32[]{:S(2)}) copy-start(bf16[69,128]{1,0:T(8,128)(2,1)} %param.14) | copy-start | bytes 52996
  30.6 22.8 %copy-start.16 = (s32[4]{0:T(128)S(1)}, s32[4]{0:T(128)}, u32[]{:S(2)}) copy-start(s32[4]{0:T(128)} %param.15) | copy-start | bytes 52
  32.3 11.1 %collective-permute-start.10 = (bf16[8,72,128]{2,1,0:T(8,128)(2,1)S(1)}, bf16[8,72,128]{2,1,0:T(8,128)(2,1)S(1)}, u32[]{:S(2)}, u32[]{:S(2)}) collective-permute-start(bf16[8,72,128]{2,1,0:T(8,128)(2,1)S(1)} %bitcast.106), channel_id=1, source_target_pairs={{0,112},{1,113},{2,114},{3,115},{4,116},{5,117},{6,118},{7,119},{8... | collective-permute-start | bytes 442376 | tf_op jit(solution)/shard_map/ppermute | solution.py:457
  38.2 8.0 %collective-permute-start.11 = (bf16[8,72,128]{2,1,0:T(8,128)(2,1)S(1)}, bf16[8,72,128]{2,1,0:T(8,128)(2,1)S(1)}, u32[]{:S(2)}, u32[]{:S(2)}) collective-permute-start(bf16[8,72,128]{2,1,0:T(8,128)(2,1)S(1)} %bitcast.108), channel_id=1, source_target_pairs={{0,120},{1,121},{2,122},{3,123},{4,124},{5,125},{6,126},{7,127},{8... | collective-permute-start | bytes 442376 | tf_op jit(solution)/shard_map/ppermute | solution.py:457
  39.3 21.1 %copy-start.6 = (bf16[80,1024]{1,0:T(8,128)(2,1)}, bf16[80,1024]{1,0:T(8,128)(2,1)S(1)}, u32[]{:S(2)}) copy-start(bf16[80,1024]{1,0:T(8,128)(2,1)S(1)} %copy.21.pay0) | copy-start | bytes 491524
  39.3 8.8 %collective-permute-start = (bf16[80,1024]{1,0:T(8,128)(2,1)S(1)}, bf16[80,1024]{1,0:T(8,128)(2,1)S(1)}, u32[]{:S(2)}, u32[]{:S(2)}) collective-permute-start(bf16[80,1024]{1,0:T(8,128)(2,1)S(1)} %copy.21.pay0), channel_id=1, source_target_pairs={{0,8},{8,16},{16,24},{24,0},{1,9},{9,17},{17,25},{25,1},{2,10},{10... | collective-permute-start | bytes 491528 | tf_op jit(solution)/shard_map/ppermute | solution.py:436
  40.3 8.6 %collective-permute-start.1 = (bf16[80,1024]{1,0:T(8,128)(2,1)S(1)}, bf16[80,1024]{1,0:T(8,128)(2,1)S(1)}, u32[]{:S(2)}, u32[]{:S(2)}) collective-permute-start(bf16[80,1024]{1,0:T(8,128)(2,1)S(1)} %copy.21.pay0), channel_id=1, source_target_pairs={{0,16},{8,24},{16,0},{24,8},{1,17},{9,25},{17,1},{25,9},{2,18},{10... | collective-permute-start | bytes 491528 | tf_op jit(solution)/shard_map/ppermute | solution.py:436
  40.3 12.6 %collective-permute-start.2 = (bf16[80,1024]{1,0:T(8,128)(2,1)S(1)}, bf16[80,1024]{1,0:T(8,128)(2,1)S(1)}, u32[]{:S(2)}, u32[]{:S(2)}) collective-permute-start(bf16[80,1024]{1,0:T(8,128)(2,1)S(1)} %copy.21.pay0), channel_id=1, source_target_pairs={{0,24},{8,0},{16,8},{24,16},{1,25},{9,1},{17,9},{25,17},{2,26},{10... | collective-permute-start | bytes 491528 | tf_op jit(solution)/shard_map/ppermute | solution.py:436
  43.3 21.2 %copy-start.15 = (bf16[72,128]{1,0:T(8,128)(2,1)}, bf16[72,128]{1,0:T(8,128)(2,1)S(1)}, u32[]{:S(2)}) copy-start(bf16[72,128]{1,0:T(8,128)(2,1)S(1)} %fusion.21.refs_14_) | copy-start | bytes 55300
  43.4 21.1 %copy-start.11 = (bf16[1,8,72,128]{3,2,1,0:T(8,128)(2,1)}, bf16[1,8,72,128]{3,2,1,0:T(8,128)(2,1)S(1)}, u32[]{:S(2)}) copy-start(bf16[1,8,72,128]{3,2,1,0:T(8,128)(2,1)S(1)} %copy.50) | copy-start | bytes 442372
  43.4 21.1 %copy-start.19 = (bf16[8,72,128]{2,1,0:T(8,128)(2,1)}, bf16[8,72,128]{2,1,0:T(8,128)(2,1)S(1)}, u32[]{:S(2)}) copy-start(bf16[8,72,128]{2,1,0:T(8,128)(2,1)S(1)} %collective-permute-done.10.refs_8_) | copy-start | bytes 442372
  43.4 21.0 %collective-permute-start.6 = (bf16[8,72,128]{2,1,0:T(8,128)(2,1)S(1)}, bf16[8,72,128]{2,1,0:T(8,128)(2,1)S(1)}, u32[]{:S(2)}, u32[]{:S(2)}) collective-permute-start(bf16[8,72,128]{2,1,0:T(8,128)(2,1)S(1)} %bitcast.107), channel_id=1, source_target_pairs={{0,16},{1,17},{2,18},{3,19},{4,20},{5,21},{6,22},{7,23},{8,24},{9,... | collective-permute-start | bytes 442376 | tf_op jit(solution)/shard_map/ppermute | solution.py:457
  46.1 18.4 %copy-start.20 = (bf16[8,72,128]{2,1,0:T(8,128)(2,1)}, bf16[8,72,128]{2,1,0:T(8,128)(2,1)S(1)}, u32[]{:S(2)}) copy-start(bf16[8,72,128]{2,1,0:T(8,128)(2,1)S(1)} %collective-permute-done.11.refs_9_) | copy-start | bytes 442372
  46.1 18.3 %collective-permute-start.7 = (bf16[8,72,128]{2,1,0:T(8,128)(2,1)S(1)}, bf16[8,72,128]{2,1,0:T(8,128)(2,1)S(1)}, u32[]{:S(2)}, u32[]{:S(2)}) collective-permute-start(bf16[8,72,128]{2,1,0:T(8,128)(2,1)S(1)} %bitcast.109), channel_id=1, source_target_pairs={{0,24},{1,25},{2,26},{3,27},{4,28},{5,29},{6,30},{7,31},{8,0},{9,1... | collective-permute-start | bytes 442376 | tf_op jit(solution)/shard_map/ppermute | solution.py:457
  48.1 12.3 %copy-start.7 = (bf16[80,1024]{1,0:T(8,128)(2,1)}, bf16[80,1024]{1,0:T(8,128)(2,1)S(1)}, u32[]{:S(2)}) copy-start(bf16[80,1024]{1,0:T(8,128)(2,1)S(1)} %collective-permute-done.pay1) | copy-start | bytes 491524
  48.1 16.3 %collective-permute-start.5 = (bf16[8,72,128]{2,1,0:T(8,128)(2,1)S(1)}, bf16[8,72,128]{2,1,0:T(8,128)(2,1)S(1)}, u32[]{:S(2)}, u32[]{:S(2)}) collective-permute-start(bf16[8,72,128]{2,1,0:T(8,128)(2,1)S(1)} %bitcast.110), channel_id=1, source_target_pairs={{0,8},{1,9},{2,10},{3,11},{4,12},{5,13},{6,14},{7,15},{8,16},{9,17... | collective-permute-start | bytes 442376 | tf_op jit(solution)/shard_map/ppermute | solution.py:457
  49.0 15.5 %collective-permute-start.9 = (bf16[8,72,128]{2,1,0:T(8,128)(2,1)S(1)}, bf16[8,72,128]{2,1,0:T(8,128)(2,1)S(1)}, u32[]{:S(2)}, u32[]{:S(2)}) collective-permute-start(bf16[8,72,128]{2,1,0:T(8,128)(2,1)S(1)} %bitcast.111), channel_id=1, source_target_pairs={{0,104},{1,105},{2,106},{3,107},{4,108},{5,109},{6,110},{7,111},{8... | collective-permute-start | bytes 442376 | tf_op jit(solution)/shard_map/ppermute | solution.py:457
  52.9 11.5 %collective-permute-start.8 = (bf16[8,72,128]{2,1,0:T(8,128)(2,1)S(1)}, bf16[8,72,128]{2,1,0:T(8,128)(2,1)S(1)}, u32[]{:S(2)}, u32[]{:S(2)}) collective-permute-start(bf16[8,72,128]{2,1,0:T(8,128)(2,1)S(1)} %bitcast.103), channel_id=1, source_target_pairs={{0,96},{1,97},{2,98},{3,99},{4,100},{5,101},{6,102},{7,103},{8,104... | collective-permute-start | bytes 442376 | tf_op jit(solution)/shard_map/ppermute | solution.py:457
  105.7 12.7 %collective-permute-start.13 = (bf16[72,3200]{1,0:T(8,128)(2,1)}, bf16[72,3200]{1,0:T(8,128)(2,1)S(1)}, u32[]{:S(2)}, u32[]{:S(2)}) collective-permute-start(bf16[72,3200]{1,0:T(8,128)(2,1)} %get-tuple-element.27), channel_id=1, source_target_pairs={{32,0},{40,8},{48,16},{56,24},{57,25},{49,17},{41,9},{33,1},{34,2}... | collective-permute-start | bytes 1382408 | tf_op jit(solution)/shard_map/ppermute | solution.py:463
  105.7 14.0 %collective-permute-start.12 = (bf16[72,3200]{1,0:T(8,128)(2,1)}, bf16[72,3200]{1,0:T(8,128)(2,1)S(1)}, u32[]{:S(2)}, u32[]{:S(2)}) collective-permute-start(bf16[72,3200]{1,0:T(8,128)(2,1)} %get-tuple-element.28), channel_id=1, source_target_pairs={{0,32},{8,40},{16,48},{24,56},{25,57},{17,49},{9,41},{1,33},{2,34}... | collective-permute-start | bytes 1382408 | tf_op jit(solution)/shard_map/ppermute | solution.py:462
  119.5 15.5 %copy-start.4 = (bf16[72,3200]{1,0:T(8,128)(2,1)}, bf16[72,3200]{1,0:T(8,128)(2,1)S(1)}, u32[]{:S(2)}) copy-start(bf16[72,3200]{1,0:T(8,128)(2,1)S(1)} %add_convert_fusion.refs_19_) | copy-start | bytes 1382404
  120.9 14.2 %copy-start.5 = (bf16[72,3200]{1,0:T(8,128)(2,1)}, bf16[72,3200]{1,0:T(8,128)(2,1)S(1)}, u32[]{:S(2)}) copy-start(bf16[72,3200]{1,0:T(8,128)(2,1)S(1)} %add_convert_fusion.1.refs_18_) | copy-start | bytes 1382404
  121.0 7.5 %collective-permute-start.14 = (bf16[72,2304]{1,0:T(8,128)(2,1)S(1)}, bf16[72,2304]{1,0:T(8,128)(2,1)S(1)}, u32[]{:S(2)}, u32[]{:S(2)}) collective-permute-start(bf16[72,2304]{1,0:T(8,128)(2,1)S(1)} %get-tuple-element.85), channel_id=1, source_target_pairs={{0,8},{8,16},{16,24},{24,25},{25,17},{17,9},{9,1},{1,2},{2,10},{10... | collective-permute-start | bytes 995336 | tf_op jit(solution)/shard_map/ppermute | solution.py:468
  123.8 11.2 %collective-permute-start.15 = (bf16[72,2304]{1,0:T(8,128)(2,1)S(1)}, bf16[72,2304]{1,0:T(8,128)(2,1)S(1)}, u32[]{:S(2)}, u32[]{:S(2)}) collective-permute-start(bf16[72,2304]{1,0:T(8,128)(2,1)S(1)} %get-tuple-element.84), channel_id=1, source_target_pairs={{8,0},{16,8},{24,16},{25,24},{17,25},{9,17},{1,9},{2,1},{10,2},{18... | collective-permute-start | bytes 995336 | tf_op jit(solution)/shard_map/ppermute | solution.py:467
  177.9 19.6 %copy-start.31 = (bf16[8,72,128]{2,1,0:T(8,128)(2,1)S(1)}, bf16[8,72,128]{2,1,0:T(8,128)(2,1)}, u32[]{:S(2)}) copy-start(bf16[8,72,128]{2,1,0:T(8,128)(2,1)} %get-tuple-element.41) | copy-start | bytes 442372
  177.9 22.8 %copy-start.30 = (bf16[8,72,128]{2,1,0:T(8,128)(2,1)S(1)}, bf16[8,72,128]{2,1,0:T(8,128)(2,1)}, u32[]{:S(2)}) copy-start(bf16[8,72,128]{2,1,0:T(8,128)(2,1)} %get-tuple-element.42) | copy-start | bytes 442372
  177.9 25.5 %copy-start.29 = (bf16[8,72,128]{2,1,0:T(8,128)(2,1)S(1)}, bf16[8,72,128]{2,1,0:T(8,128)(2,1)}, u32[]{:S(2)}) copy-start(bf16[8,72,128]{2,1,0:T(8,128)(2,1)} %get-tuple-element.43) | copy-start | bytes 442372
  177.9 25.5 %copy-start.28 = (bf16[8,72,128]{2,1,0:T(8,128)(2,1)S(1)}, bf16[8,72,128]{2,1,0:T(8,128)(2,1)}, u32[]{:S(2)}) copy-start(bf16[8,72,128]{2,1,0:T(8,128)(2,1)} %get-tuple-element.44) | copy-start | bytes 442372
  177.9 29.2 %copy-start.27 = (bf16[8,72,128]{2,1,0:T(8,128)(2,1)S(1)}, bf16[8,72,128]{2,1,0:T(8,128)(2,1)}, u32[]{:S(2)}) copy-start(bf16[8,72,128]{2,1,0:T(8,128)(2,1)} %get-tuple-element.45) | copy-start | bytes 442372
  177.9 29.2 %copy-start.12 = (bf16[8,72,128]{2,1,0:T(8,128)(2,1)S(1)}, bf16[8,72,128]{2,1,0:T(8,128)(2,1)}, u32[]{:S(2)}) copy-start(bf16[8,72,128]{2,1,0:T(8,128)(2,1)} %get-tuple-element.39) | copy-start | bytes 442372
  178.0 39.3 %copy-start.26 = (bf16[8,72,128]{2,1,0:T(8,128)(2,1)S(1)}, bf16[8,72,128]{2,1,0:T(8,128)(2,1)}, u32[]{:S(2)}) copy-start(bf16[8,72,128]{2,1,0:T(8,128)(2,1)} %get-tuple-element.46) | copy-start | bytes 442372
  181.7 25.5 %collective-permute-start.16 = (bf16[8,72,128]{2,1,0:T(8,128)(2,1)}, bf16[8,72,128]{2,1,0:T(8,128)(2,1)S(1)}, u32[]{:S(2)}, u32[]{:S(2)}) collective-permute-start(bf16[8,72,128]{2,1,0:T(8,128)(2,1)} %get-tuple-element.40), channel_id=1, source_target_pairs={{96,0},{97,1},{98,2},{99,3},{100,4},{101,5},{102,6},{103,7},{104,8... | collective-permute-start | bytes 442376 | tf_op jit(solution)/shard_map/ppermute | solution.py:488
  185.5 55.2 %all-to-all-start.1 = ((bf16[72,128,32]{0,2,1:T(8,128)(2,1)}), bf16[72,128,32]{0,2,1:T(8,128)(2,1)S(1)}, u32[]{:S(2)}, u32[]{:S(2)}) async-start(bf16[72,128,32]{0,2,1:T(8,128)(2,1)} %bitcast.53), calls=%async_computation.1 | async-start | bytes 2097152 | tf_op jit(solution)/shard_map/all_to_all | solution.py:480
  197.5 19.8 %collective-permute-start.17 = (bf16[8,72,128]{2,1,0:T(8,128)(2,1)S(1)}, bf16[8,72,128]{2,1,0:T(8,128)(2,1)S(1)}, u32[]{:S(2)}, u32[]{:S(2)}) collective-permute-start(bf16[8,72,128]{2,1,0:T(8,128)(2,1)S(1)} %copy-done.31), channel_id=1, source_target_pairs={{8,0},{9,1},{10,2},{11,3},{12,4},{13,5},{14,6},{15,7},{16,8},{17,9... | collective-permute-start | bytes 442376 | tf_op jit(solution)/shard_map/ppermute | solution.py:488
  200.7 21.5 %collective-permute-start.18 = (bf16[8,72,128]{2,1,0:T(8,128)(2,1)S(1)}, bf16[8,72,128]{2,1,0:T(8,128)(2,1)S(1)}, u32[]{:S(2)}, u32[]{:S(2)}) collective-permute-start(bf16[8,72,128]{2,1,0:T(8,128)(2,1)S(1)} %copy-done.30), channel_id=1, source_target_pairs={{104,0},{105,1},{106,2},{107,3},{108,4},{109,5},{110,6},{111,7},{1... | collective-permute-start | bytes 442376 | tf_op jit(solution)/shard_map/ppermute | solution.py:488
  203.4 20.6 %collective-permute-start.19 = (bf16[8,72,128]{2,1,0:T(8,128)(2,1)S(1)}, bf16[8,72,128]{2,1,0:T(8,128)(2,1)S(1)}, u32[]{:S(2)}, u32[]{:S(2)}) collective-permute-start(bf16[8,72,128]{2,1,0:T(8,128)(2,1)S(1)} %copy-done.29), channel_id=1, source_target_pairs={{16,0},{17,1},{18,2},{19,3},{20,4},{21,5},{22,6},{23,7},{24,8},{25... | collective-permute-start | bytes 442376 | tf_op jit(solution)/shard_map/ppermute | solution.py:488
  203.4 20.6 %collective-permute-start.20 = (bf16[8,72,128]{2,1,0:T(8,128)(2,1)S(1)}, bf16[8,72,128]{2,1,0:T(8,128)(2,1)S(1)}, u32[]{:S(2)}, u32[]{:S(2)}) collective-permute-start(bf16[8,72,128]{2,1,0:T(8,128)(2,1)S(1)} %copy-done.28), channel_id=1, source_target_pairs={{112,0},{113,1},{114,2},{115,3},{116,4},{117,5},{118,6},{119,7},{1... | collective-permute-start | bytes 442376 | tf_op jit(solution)/shard_map/ppermute | solution.py:488
  207.2 19.0 %collective-permute-start.21 = (bf16[8,72,128]{2,1,0:T(8,128)(2,1)S(1)}, bf16[8,72,128]{2,1,0:T(8,128)(2,1)S(1)}, u32[]{:S(2)}, u32[]{:S(2)}) collective-permute-start(bf16[8,72,128]{2,1,0:T(8,128)(2,1)S(1)} %copy-done.27), channel_id=1, source_target_pairs={{24,0},{25,1},{26,2},{27,3},{28,4},{29,5},{30,6},{31,7},{0,8},{1,9... | collective-permute-start | bytes 442376 | tf_op jit(solution)/shard_map/ppermute | solution.py:488
  217.2 8.9 %collective-permute-start.22 = (bf16[8,72,128]{2,1,0:T(8,128)(2,1)S(1)}, bf16[8,72,128]{2,1,0:T(8,128)(2,1)S(1)}, u32[]{:S(2)}, u32[]{:S(2)}) collective-permute-start(bf16[8,72,128]{2,1,0:T(8,128)(2,1)S(1)} %copy-done.26), channel_id=1, source_target_pairs={{120,0},{121,1},{122,2},{123,3},{124,4},{125,5},{126,6},{127,7},{9... | collective-permute-start | bytes 442376 | tf_op jit(solution)/shard_map/ppermute | solution.py:488
  226.3 13.2 %copy-start.3 = (f32[69,8,256]{2,1,0:T(8,128)S(1)}, f32[69,8,256]{2,1,0:T(8,128)}, u32[]{:S(2)}) copy-start(f32[69,8,256]{2,1,0:T(8,128)} %param.11) | copy-start | bytes 1695748
  226.8 14.0 %copy-start.10 = (f32[69,512]{1,0:T(8,128)S(1)}, f32[69,512]{1,0:T(8,128)}, u32[]{:S(2)}) copy-start(f32[69,512]{1,0:T(8,128)} %param.16) | copy-start | bytes 423940
  226.9 7.9 %collective-permute-start.23 = (bf16[8,72,32]{2,1,0:T(8,128)(2,1)S(1)}, bf16[8,72,32]{2,1,0:T(8,128)(2,1)S(1)}, u32[]{:S(2)}, u32[]{:S(2)}) collective-permute-start(bf16[8,72,32]{2,1,0:T(8,128)(2,1)S(1)} %get-tuple-element.74), channel_id=1, source_target_pairs={{0,1},{1,2},{2,3},{3,4},{4,5},{5,6},{6,7},{8,9},{9,10},{10,11},{11... | collective-permute-start | bytes 110600 | tf_op jit(solution)/shard_map/ppermute | solution.py:495
  230.4 9.1 %collective-permute-start.24 = (bf16[8,72,32]{2,1,0:T(8,128)(2,1)S(1)}, bf16[8,72,32]{2,1,0:T(8,128)(2,1)S(1)}, u32[]{:S(2)}, u32[]{:S(2)}) collective-permute-start(bf16[8,72,32]{2,1,0:T(8,128)(2,1)S(1)} %get-tuple-element.75), channel_id=1, source_target_pairs={{1,0},{2,1},{3,2},{4,3},{5,4},{6,5},{7,6},{9,8},{10,9},{11,10},{12... | collective-permute-start | bytes 110600 | tf_op jit(solution)/shard_map/ppermute | solution.py:496
  (11 other events, 34.0 us)
where the time goes:
time: 240 us; the launch traced here: 242 us
  Pallas kernels  90.1 us (38%)
  starting transfers between devices  73.1 us (30%)
  waiting for transfers between devices  43.3 us (18%)
  other arithmetic  14.8 us (6%)
  local copies, waits for them, and re-layouts  13.2 us (6%)
  between operations  5.47 us (2%)
    pallas_call x2, Pallas kernels, iteration(): pl.pallas_call(functools.partial(iterate, second), out_shape=shapes, in_s...  82.5 us
    ppermute x7, starting transfers between devices, on_device(): lax.ppermute(moves[m], AXES, [(b, a) for a, b in family(m)])  16.3 us
    ppermute x7, waiting for transfers between devices, on_device(): lax.ppermute(moves[m], AXES, [(b, a) for a, b in family(m)])  13.9 us
    ppermute x7, starting transfers between devices, on_device(): lax.ppermute(sends[m % 4], AXES, family(m))  13.1 us
    all_to_all x1, starting transfers between devices, on_device(): lax.all_to_all(spread, AXES, split_axis=1, concat_axis=1, tiled=True)  12 us
    ppermute x1, waiting for transfers between devices, on_device(): right_in = lax.ppermute(left, AXES, LON_DOWN)  10.7 us
    all_to_all x1, starting transfers between devices, on_device(): lax.all_to_all(packed, AXES, split_axis=1, concat_axis=1, tiled=True, axi...  9.38 us
    ppermute x1, waiting for transfers between devices, on_device(): lax.ppermute(jnp.concatenate([left[:, 0:1024], right[:, 0:1024]] + extra,...  6.6 us
  transfers between devices with their start and end apart: 27, of which 11 were waited for; matrix products, arithmetic and copies ran while one was open for 10% of the time, Pallas kernels for 2%

commit v1 on v0

--- a/solution.py
+++ b/solution.py
@@ -51,6 +51,10 @@
     return pairs
 
 
+def turn(m):
+    return [(g[s], g[(s + m) % 4]) for g in GROUPS_4 for s in range(4)]
+
+
 def nt(a, b):
     return lax.dot_general(a, b, (((1,), (1,)), ((), ())), preferred_element_type=F32)
 
@@ -61,6 +65,50 @@
 
 def nn(a, b):
     return jnp.dot(a, b, preferred_element_type=F32)
+
+
+def pack_kernel(values, prec, frac, dest, cell, packed, slots):
+    rows = dest.shape[1]
+    owner = dest[...]
+    group = lax.shift_right_logical(owner, 5) * 8 + (owner & 7)
+    member = lax.broadcasted_iota(jnp.int32, (32, rows), 0) == group
+    row = lax.broadcasted_iota(jnp.int32, (rows, rows), 0)
+    col = lax.broadcasted_iota(jnp.int32, (rows, rows), 1)
+    before = nn(jnp.where(member, 1.0, 0.0).astype(BF), jnp.where(row < col, 1.0, 0.0).astype(BF))
+    rank = jnp.sum(jnp.where(member, before, 0.0), axis=0, keepdims=True)
+    slot = group * 32 + rank.astype(jnp.int32)
+    slots[...] = slot
+    lon = jnp.zeros((1, rows), F32)
+    code = cell[...]
+    for step in range(1, 7):
+        lon = lon + jnp.where(code >= 255 * step, 1.0, 0.0)
+    lat = code.astype(F32) - 255.0 * lon
+    lon = lon + 8.0 * (lax.shift_right_logical(owner, 3) & 3).astype(F32)
+    parts = []
+    for x in (prec[...], frac[0:1], frac[1:2]):
+        high = x.astype(BF).astype(F32)
+        parts += [high, x - high]
+    ctrl = jnp.concatenate(parts + [lon, lat], axis=0)
+    payload = jnp.concatenate([values[...], jnp.zeros((3, rows), F32), ctrl], axis=0).astype(BF)
+    for c in range(4):
+        index = lax.broadcasted_iota(jnp.int32, (256, rows), 0) + 256 * c
+        pick = jnp.where(index == slot, 1.0, 0.0).astype(BF)
+        packed[:, 256 * c : 256 * c + 256] = nt(payload, pick).astype(BF)
+
+
+def split_kernel(scal, cells, before, after, *outs):
+    for b in range(4):
+        for m in range(4):
+            @pl.when(scal[20 + m] == b)
+            def _():
+                for r in range(8):
+                    if b == 0:
+                        x = jnp.concatenate([before[r], cells[r, :, 0:96]], axis=1)
+                    elif b == 3:
+                        x = jnp.concatenate([cells[r, :, 160:256], after[r]], axis=1)
+                    else:
+                        x = cells[r, :, 64 * b - 32 : 64 * b + 96]
+                    outs[m][r] = x
 
 
 def compact_kernel(scal, pay0, pay1, pay2, pay3, comp, posx, count, total):
@@ -85,7 +133,8 @@
     place = before + offset
     owned = jnp.where(own > 0.0, place, -1.0)
     for m in range(4):
-        posx[pl.ds(pl.multiple_of(8 * (scal[8 + m] - 2), 8), 8), :] = owned[8 * m : 8 * m + 8]
+        to = 8 * ((4 - m) % 4)
+        posx[to : to + 8, :] = owned[8 * m : 8 * m + 8]
     total[...] = jnp.where(mine > 0.0, place, -1.0)
     number = jnp.sum(mine).astype(jnp.int32)
     count[0] = number
@@ -104,7 +153,8 @@
         comp[:, pl.ds(pl.multiple_of(tile * 256, 256), 256)] = out.astype(BF)
 
 
-def expand_kernel(count, posx, found, out, total):
+def expand_kernel(count, posx, found, *refs):
+    outs, total = refs[0:4], refs[4]
     index = lax.broadcasted_iota(jnp.int32, (256, 128), 0).astype(F32)
     total[...] = jnp.zeros_like(total)
 
@@ -114,10 +164,10 @@
         rows = found[:, pl.ds(pl.multiple_of(tile * 256, 256), 256)]
         for c in range(32):
             picks = jnp.where(ids == posx[c : c + 1, :], 1.0, 0.0).astype(BF)
-            to = 128 * (8 * (c % 8 // 2) + 2 * (c // 8) + c % 2)
-            total[:, to : to + 128] += nn(rows, picks)
-
-    out[...] = total[...].astype(BF)
+            total[:, 128 * c : 128 * c + 128] += nn(rows, picks)
+
+    for m in range(4):
+        outs[m][...] = total[:, 1024 * m : 1024 * m + 1024].astype(BF)
 
 
 def convolve(act, weight, d, first, count, store):
@@ -141,8 +191,8 @@
 def iterate(second, *refs):
     scal, count = refs[0:2]
     chunks = refs[2:10]
-    enc_t, enc_eye, dec_eye, dec_n, eye, wf, wb, comp = refs[10:18]
-    refs = refs[18:]
+    enc_eye, dec_eye, dec_n, wf, wb, comp = refs[10:16]
+    refs = refs[16:]
     if second:
         tots, from_prev, from_next = refs[0:2], refs[2], refs[3]
         outs, found = refs[4:12], refs[12]
@@ -152,17 +202,19 @@
         refs = refs[2:]
     st, h, act, slope, bk, fct, wobs, g, ga, shift = refs
 
-    act[...] = jnp.zeros_like(act)
+    act[60:96] = jnp.zeros((36, 96, 384), BF)
 
     for f in range(8):
         base = 8 * scal[8 + f]
         for r in range(8):
-            st[base + r] = tn(chunks[f][r], eye[...])
+            both = tn(chunks[f][r], enc_eye[...])
+            h[base + r + OFF] = both[:, 0:128]
+            st[base + r] = both[16:112, 128:256]
     if second:
         for half in range(2):
             tot = tots[half]
             for c in range(2):
-                rows = pl.ds(32 * half + 16 * c, 16)
+                row = 32 * half + 16 * c
                 lanes = 1024 * half + 512 * c
                 for sec in range(3):
                     add = tot[:, 1024 * sec + 512 * c : 1024 * sec + 512 * c + 512].astype(F32)
@@ -170,20 +222,16 @@
                         add = add + from_prev[:, lanes : lanes + 512].astype(F32)
                     if sec == 2:
                         add = add + from_next[:, lanes : lanes + 512].astype(F32)
-                    add = tn(add.astype(BF), eye[...]).reshape(16, 32, 128)
-                    st[rows, 16 + 32 * sec : 48 + 32 * sec, :] -= STEP * add
+                    both = tn(add.astype(BF), enc_eye[...]).reshape(16, 32, 256)
+                    h[row + OFF : row + OFF + 16, 16 + 32 * sec : 48 + 32 * sec, :] -= STEP * both[:, :, 0:128]
                     if half + c == 1:
-                        ga[pl.ds(16 * c_own(half, c), 16), 32 * sec : 32 * sec + 32, :] = 0.75 * add
-            low = tn(from_prev[:, 2048 + 128 * half : 2176 + 128 * half], eye[...])
-            high = tn(from_next[:, 2048 + 128 * half : 2176 + 128 * half], eye[...])
+                        st[row : row + 16, 32 * sec : 32 + 32 * sec, :] -= STEP * both[:, :, 128:256]
+                        ga[row - 16 : row, 32 * sec : 32 * sec + 32, :] = 0.75 * both[:, :, 128:256]
+            low = tn(from_prev[:, 2048 + 128 * half : 2176 + 128 * half], enc_eye[:, 0:128])
+            high = tn(from_next[:, 2048 + 128 * half : 2176 + 128 * half], enc_eye[:, 0:128])
             for i in range(32):
-                st[32 * half + i, 15:16, :] -= STEP * low[32 + i : 33 + i]
-                st[32 * half + i, 112:113, :] -= STEP * high[i : i + 1]
-
-    @pl.loop(0, 8)
-    def _(c):
-        x = st[pl.ds(8 * c, 8)].reshape(1024, 128).astype(BF)
-        h[pl.ds(8 * c + OFF, 8)] = nn(x, enc_t[...]).reshape(8, 128, 128)
+                h[32 * half + i + OFF, 15:16, :] -= STEP * low[32 + i : 33 + i]
+                h[32 * half + i + OFF, 112:113, :] -= STEP * high[i : i + 1]
 
     e = lax.broadcasted_iota(jnp.int32, (112, 128), 0) + 8
     mask = jnp.where((e >= scal[4]) & (e < scal[5]), 1.0, 0.0)
@@ -215,7 +263,7 @@
 
     for c in range(4):
         a = h[16 + OFF + 8 * c : 24 + OFF + 8 * c, 16:112, :].reshape(768, 128).astype(BF)
-        b = st[16 + 8 * c : 24 + 8 * c, 16:112, :].reshape(768, 128).astype(BF)
+        b = st[16 + 8 * c : 24 + 8 * c].reshape(768, 128).astype(BF)
         fct[:, 768 * c : 768 * c + 768] = nt(dec_eye[...], jnp.concatenate([a, b], axis=1)).astype(BF)
 
     g[...] = jnp.zeros_like(g)
@@ -315,10 +363,6 @@
             outs[half][:, 3072:3200] = nt(enc_eye[...], x).astype(BF)
 
 
-def c_own(half, c):
-    return 0 if (half, c) == (0, 1) else 1
-
-
 def iteration(second, scal, count, *arrays):
     smem = pl.BlockSpec(memory_space=pltpu.SMEM)
     vmem = pl.BlockSpec(memory_space=pltpu.VMEM)
@@ -332,7 +376,7 @@
         in_specs=[smem, smem] + [vmem] * len(arrays),
         out_specs=[vmem] * len(shapes),
         scratch_shapes=[
-            pltpu.VMEM((64, 128, 128), F32),
+            pltpu.VMEM((64, 96, 128), F32),
             pltpu.VMEM((ROWS, 128, 128), F32),
             pltpu.VMEM((ROWS, 96, 384), BF),
             pltpu.VMEM((4, ROWS, 96, 128), BF),
@@ -364,11 +408,9 @@
     ahead = convolution_weight.transpose(0, 1, 3, 2).reshape(4, 3, 384, 128)
     back = convolution_weight[:, ::-1].reshape(4, 3, 384, 128)
     return (
-        enc_v,
         jnp.concatenate([enc_v[0:V], eye], axis=1),
         jnp.concatenate([dec_v[0:V], eye], axis=1),
         dec_v,
-        eye,
         paired(ahead),
         paired(back),
     )
@@ -405,36 +447,33 @@
         [d[0], d[1], d[2], d[3], 32 - top, 2048 + 32 - top, 64 * k, jnp.int32(0)]
         + tables
         + [d[1] + d[2] + d[3], d[2] + d[3], d[3], jnp.int32(0)]
+        + [block_of((sub + m) % 4) for m in range(4)]
     ).astype(jnp.int32)
 
+    cells = jnp.pad(background.astype(BF).transpose(1, 0, 2), ((0, 0), (0, V - 69), (0, 0)))
+    before = lax.ppermute(cells[:, :, 224:256], AXES, BAND_UP)
+    after = lax.ppermute(cells[:, :, 0:32], AXES, BAND_DOWN)
+    sends = pl.pallas_call(
+        split_kernel,
+        out_shape=[jax.ShapeDtypeStruct((8, V, 128), BF)] * 4,
+        in_specs=[smem] + [vmem] * 3,
+        out_specs=[vmem] * 4,
+        name="split",
+    )(scal, cells, before, after)
+    chunks = [sends[0]] + [lax.ppermute(sends[m % 4], AXES, family(m)) for m in range(1, 8)]
+
     rows = obs_dest.shape[0]
-    owner = obs_dest[:, 0]
-    group = (owner // 32) * 8 + owner % 8
-    member = (group[:, None] == jnp.arange(32, dtype=jnp.int32)[None, :]).astype(BF)
-    order = jnp.arange(rows, dtype=jnp.int32)
-    earlier = (order[None, :] < order[:, None]).astype(BF)
-    rank = jnp.sum(nn(earlier, member) * member.astype(F32), axis=1).astype(jnp.int32)
-    slots = group * 32 + rank
     alive = (jnp.arange(rows, dtype=jnp.int32) < obs_count[0]).astype(F32)
-    prec = alive * obs_prec
-    wide = jnp.stack([prec, obs_frac[0], obs_frac[1]])
-    high = wide.astype(BF)
-    low = (wide - high.astype(F32)).astype(BF)
-    li = 8 * ((owner // 8) % 4) + obs_cell // 255
-    lj = obs_cell % 255
-    payload = jnp.concatenate(
-        [
-            obs_values.astype(BF),
-            jnp.zeros((3, rows), BF),
-            jnp.stack([high[0], low[0], high[1], low[1], high[2], low[2], li.astype(BF), lj.astype(BF)]),
-        ]
-    )
-    pick = (slots[:, None] == jnp.arange(1024, dtype=jnp.int32)[None, :]).astype(BF)
-    packed = jnp.einsum("vr,rs->vs", payload, pick, preferred_element_type=F32).astype(BF)
+    packed, slots = pl.pallas_call(
+        pack_kernel,
+        out_shape=[jax.ShapeDtypeStruct((80, 1024), BF), jax.ShapeDtypeStruct((1, rows), jnp.int32)],
+        in_specs=[vmem] * 5,
+        out_specs=[vmem] * 2,
+        name="pack",
+    )(obs_values, (alive * obs_prec)[None, :], obs_frac, obs_dest.reshape(1, rows), obs_cell[None, :])
+    pick = (slots.reshape(rows, 1) == jnp.arange(1024, dtype=jnp.int32)[None, :]).astype(BF)
     arrived = lax.all_to_all(packed, AXES, split_axis=1, concat_axis=1, tiled=True, axis_index_groups=GROUPS_32)
-    others = [
-        lax.ppermute(arrived, AXES, [(g[s], g[(s + m) % 4]) for g in GROUPS_4 for s in range(4)]) for m in range(1, 4)
-    ]
+    others = [lax.ppermute(arrived, AXES, turn(m)) for m in range(1, 4)]
     comp, posx, count = pl.pallas_call(
         compact_kernel,
         out_shape=[
@@ -448,14 +487,6 @@
         name="compact",
     )(scal, arrived, *others)
 
-    cells = jnp.pad(background.astype(BF).transpose(1, 0, 2), ((0, 0), (0, V - 69), (0, 0)))
-    before = lax.ppermute(cells[:, :, 224:256], AXES, BAND_UP)
-    after = lax.ppermute(cells[:, :, 0:32], AXES, BAND_DOWN)
-    band = jnp.concatenate([before, cells, after], axis=2)
-    parts = jnp.stack([band[:, :, 64 * b : 64 * b + 128] for b in range(4)])
-    sends = [lax.dynamic_index_in_dim(parts, block_of((sub + m) % 4), 0, keepdims=False) for m in range(4)]
-    chunks = [sends[0]] + [lax.ppermute(sends[m % 4], AXES, family(m)) for m in range(1, 8)]
-
     weights = make_weights(encoder_weight, convolution_weight, decoder_weight)
 
     left, right = iteration(False, scal, count, *chunks, *weights, comp)
@@ -470,18 +501,18 @@
 
     spread = pl.pallas_call(
         expand_kernel,
-        out_shape=jax.ShapeDtypeStruct((V, 4096), BF),
+        out_shape=[jax.ShapeDtypeStruct((V, 1024), BF)] * 4,
         in_specs=[smem, vmem, vmem],
-        out_specs=vmem,
+        out_specs=[vmem] * 4,
         scratch_shapes=[pltpu.VMEM((V, 4096), F32)],
         name="expand",
     )(count, posx, found)
-    *moves, spread = lax.optimization_barrier((*moves, spread))
-    spread = lax.all_to_all(spread, AXES, split_axis=1, concat_axis=1, tiled=True)
-    spread = [spread[:, 256 * c : 256 * c + 256] for c in range(16)]
-    spread = jnp.concatenate(
-        [spread[4 * y] + spread[4 * y + 1] + spread[4 * y + 2] + spread[4 * y + 3] for y in range(4)], axis=1
-    )
+    moves = lax.optimization_barrier((*moves, *spread))
+    moves, spread = moves[0:8], moves[8:12]
+    parts = [lax.ppermute(spread[m], AXES, turn(m)) for m in range(1, 4)]
+    parts = [p.astype(F32) for p in [spread[0]] + parts]
+    spread = (parts[0] + parts[1] + parts[2] + parts[3]).astype(BF)
+    spread = lax.all_to_all(spread, AXES, split_axis=1, concat_axis=1, tiled=True, axis_index_groups=GROUPS_32)
     equivalent = jnp.einsum("vs,rs->vr", spread[0:69], pick, preferred_element_type=F32)
     innovation = alive[None, :] * (equivalent - obs_values)
 

time: 240 us -> 237 us (0.988); the launches traced: 242 us -> 233 us
  Pallas kernels: 90.1 us -> 86 us
  starting transfers between devices: 73.1 us -> 69.3 us
    pallas_call x2, Pallas kernels: 82.5 us -> 73.5 us  [iteration(): pl.pallas_call(functools.partial(iterate, second), out_shape=shapes, in_s...]
    ppermute x7, starting transfers between devices: 16.3 us -> 10.3 us  [on_device(): lax.ppermute(moves[m], AXES, [(b, a) for a, b in family(m)])]
    all_to_all x1, waiting for transfers between devices: 0.01 us -> 5.56 us  [on_device(): lax.all_to_all(spread, AXES, split_axis=1, concat_axis=1, tiled=True, axi...]
    ppermute x1, waiting for transfers between devices: 4.69 us -> 0.01 us  [on_device(): edge_down = lax.ppermute(total[:, :, 0:32].astype(BF), AXES, BAND_DOWN)]
    pallas_call x1 -> x3, Pallas kernels: 3.7 us -> 8.37 us  [the longest x1 3.56 us: on_device(): pl.pallas_call(expand_kernel, out_shape=[jax.ShapeDtypeStruct((V, 1024),...]
    ppermute x3 -> x6, starting transfers between devices: 3.91 us -> 8.4 us  [the longest x3 4.47 us: on_device(): parts = [lax.ppermute(spread[m], AXES, turn(m)) for m in range(1, 4)]]
    all_to_all x1, starting transfers between devices: 12 us -> 8.17 us  [on_device(): lax.all_to_all(spread, AXES, split_axis=1, concat_axis=1, tiled=True, axi...]
    ppermute x1, starting transfers between devices: 0.01 us -> 3.7 us  [on_device(): right_in = lax.ppermute(left, AXES, LON_DOWN)]
  transfers between devices with their start and end apart: 27 -> 30, of which waited for: 11 -> 12; matrix products, arithmetic and copies ran while one was open for 10% -> 9% of each run, Pallas kernels for 2% -> 4%
where the time goes in v1:
time: 237 us; the launch traced here: 233 us
  Pallas kernels  86 us (36%)
  starting transfers between devices  69.3 us (29%)
  waiting for transfers between devices  45.1 us (19%)
  local copies, waits for them, and re-layouts  13.8 us (6%)
  other arithmetic  12.6 us (5%)
  between operations  5.2 us (2%)
    pallas_call x2, Pallas kernels, iteration(): pl.pallas_call(functools.partial(iterate, second), out_shape=shapes, in_s...  73.5 us
    ppermute x7, waiting for transfers between devices, on_device(): lax.ppermute(moves[m], AXES, [(b, a) for a, b in family(m)])  16.7 us
    ppermute x7, starting transfers between devices, on_device(): lax.ppermute(sends[m % 4], AXES, family(m))  12.6 us
    ppermute x7, starting transfers between devices, on_device(): lax.ppermute(moves[m], AXES, [(b, a) for a, b in family(m)])  10.3 us
    ppermute x1, waiting for transfers between devices, on_device(): right_in = lax.ppermute(left, AXES, LON_DOWN)  10.1 us
    all_to_all x1, starting transfers between devices, on_device(): lax.all_to_all(packed, AXES, split_axis=1, concat_axis=1, tiled=True, axi...  9.36 us
    all_to_all x1, starting transfers between devices, on_device(): lax.all_to_all(spread, AXES, split_axis=1, concat_axis=1, tiled=True, axi...  8.17 us
    ppermute x1, waiting for transfers between devices, on_device(): lax.ppermute(jnp.concatenate([left[:, 0:1024], right[:, 0:1024]] + extra,...  6.6 us
  transfers between devices with their start and end apart: 30, of which 12 were waited for; matrix products, arithmetic and copies ran while one was open for 9% of the time, Pallas kernels for 4%

profile of v1, /device:TPU:6, one launch (start us, length us, event | category | flops | bytes accessed | tf_op | source)
XLA Modules:
  0.0 233.3 jit_solution(7976557670258284953)
XLA Ops:
  0.6 1.2 convert_element_type.94
  3.4 3.7 %collective-permute-start.3 = (bf16[8,72,32]{2,1,0:T(8,128)(2,1)}, bf16[8,72,32]{2,1,0:T(8,128)(2,1)}, u32[]{:S(2)}, u32[]{:S(2)}) collective-permute-start(bf16[8,72,32]{2,1,0:T(8,128)(2,1)} %get-tuple-element.99), channel_id=1, source_target_pairs={{0,1},{1,2},{2,3},{3,4},{4,5},{5,6},{6,7},{8,9},{9,10},{10,11},{11... | collective-permute-start | bytes 110600 | tf_op jit(solution)/shard_map/ppermute | solution.py:454
  7.1 2.1 collective-permute-start.4
  9.9 1.3 fusion.15
  11.2 2.3 pack.1
  13.4 1.8 copy.30
  15.2 9.4 %all-to-all-start = ((bf16[80,32,32]{0,2,1:T(8,128)(2,1)}), bf16[80,32,32]{0,2,1:T(8,128)(2,1)}, u32[]{:S(2)}, u32[]{:S(2)}) async-start(bf16[80,32,32]{0,2,1:T(8,128)(2,1)} %bitcast.24), calls=%async_computation | async-start | bytes 524288 | tf_op jit(solution)/shard_map/all_to_all | solution.py:475
  25.4 1.2 slice_bitcast_fusion.2
  31.4 1.4 stack.86.scal.refs_0_
  32.8 2.5 %split.1 = (bf16[8,72,128]{2,1,0:T(8,128)(2,1)}, bf16[8,72,128]{2,1,0:T(8,128)(2,1)}, bf16[8,72,128]{2,1,0:T(8,128)(2,1)}, bf16[8,72,128]{2,1,0:T(8,128)(2,1)}) custom-call(s32[24]{0:T(128)} %stack.86.scal.refs_0_, bf16[8,72,256]{2,1,0:T(8,128)(2,1)} %pad.41.cells, bf16[8,72,32]{2,1,0:T(8,128)(2,1)} %collective-permute-done.3.before, ...), custom_call_target="tpu_custom_call" | custom-call | tf_op jit(solution)/shard_map/split/pallas_call | solution.py:456
  35.3 5.8 %collective-permute-start.10 = (bf16[8,72,128]{2,1,0:T(8,128)(2,1)}, bf16[8,72,128]{2,1,0:T(8,128)(2,1)S(1)}, u32[]{:S(2)}, u32[]{:S(2)}) collective-permute-start(bf16[8,72,128]{2,1,0:T(8,128)(2,1)} %get-tuple-element.42), channel_id=1, source_target_pairs={{0,112},{1,113},{2,114},{3,115},{4,116},{5,117},{6,118},{7,119},{8... | collective-permute-start | bytes 442376 | tf_op jit(solution)/shard_map/ppermute | solution.py:463
  41.1 1.1 copy.34.pay0
  42.2 1.0 collective-permute-start
  43.2 2.9 %collective-permute-start.2 = (bf16[80,1024]{1,0:T(8,128)(2,1)S(1)}, bf16[80,1024]{1,0:T(8,128)(2,1)S(1)}, u32[]{:S(2)}, u32[]{:S(2)}) collective-permute-start(bf16[80,1024]{1,0:T(8,128)(2,1)S(1)} %copy.34.pay0), channel_id=1, source_target_pairs={{0,24},{8,0},{16,8},{24,16},{1,25},{9,1},{17,9},{25,17},{2,26},{10... | collective-permute-start | bytes 491528 | tf_op jit(solution)/shard_map/ppermute | solution.py:476
  46.2 5.4 %fusion.1 = (bf16[4,1536,256]{2,1,0:T(8,128)(2,1)}, bf16[4,1536,256]{2,1,0:T(8,128)(2,1)}) fusion(bf16[4,384,128]{2,1,0:T(8,128)(2,1)S(1)} %broadcast.42, bf16[4,384,128]{2,1,0:T(8,128)(2,1)} %get-tuple-element.86, bf16[4,384,128]{2,1,0:T(8,128)(2,1)S(1)} %get-tuple-element.85, bf16[4,384,128]{2,1,0:T(8,128)(2,1)S(1)} %get-tuple-element.84, ...), kind=kLoop, calls=%fused_computation.5 | loop fusion | flops 47185920 | bytes 9043968 | tf_op jit(solution)/shard_map/concatenate | solution.py:401
  51.7 2.7 %collective-permute-start.6 = (bf16[8,72,128]{2,1,0:T(8,128)(2,1)S(1)}, bf16[8,72,128]{2,1,0:T(8,128)(2,1)S(1)}, u32[]{:S(2)}, u32[]{:S(2)}) collective-permute-start(bf16[8,72,128]{2,1,0:T(8,128)(2,1)S(1)} %copy-done.27), channel_id=1, source_target_pairs={{0,16},{1,17},{2,18},{3,19},{4,20},{5,21},{6,22},{7,23},{8,24},{9,... | collective-permute-start | bytes 442376 | tf_op jit(solution)/shard_map/ppermute | solution.py:463
  55.0 3.5 %collective-permute-start.9 = (bf16[8,72,128]{2,1,0:T(8,128)(2,1)S(1)}, bf16[8,72,128]{2,1,0:T(8,128)(2,1)S(1)}, u32[]{:S(2)}, u32[]{:S(2)}) collective-permute-start(bf16[8,72,128]{2,1,0:T(8,128)(2,1)S(1)} %copy-done.25), channel_id=1, source_target_pairs={{0,104},{1,105},{2,106},{3,107},{4,108},{5,109},{6,110},{7,111},{8... | collective-permute-start | bytes 442376 | tf_op jit(solution)/shard_map/ppermute | solution.py:463
  59.9 4.1 %compact.1 = (bf16[80,4096]{1,0:T(8,128)(2,1)}, f32[32,128]{1,0:T(8,128)}, s32[1]{0:T(128)}) custom-call(s32[24]{0:T(128)} %stack.86.scal.refs_0_, bf16[80,1024]{1,0:T(8,128)(2,1)} %copy-done.6, bf16[80,1024]{1,0:T(8,128)(2,1)} %copy-done.7, bf16[80,1024]{1,0:T(8,128)(2,1)} %copy-done.8, bf16[80,1024]{1,0:T(8,128)(2,1)} %copy-done.9), custom_call_target="tpu_custom_call" | custom-call | tf_op jit(solution)/shard_map/compact/pallas_call | solution.py:477
  64.1 1.5 collective-permute-done.8.refs_6_
  66.3 35.8 %first_iteration.1 = (bf16[72,3200]{1,0:T(8,128)(2,1)}, bf16[72,3200]{1,0:T(8,128)(2,1)}) custom-call(s32[24]{0:T(128)} %stack.86.scal.refs_0_, s32[1]{0:T(128)} %get-tuple-element.39.refs_1_.count, bf16[8,72,128]{2,1,0:T(8,128)(2,1)} %get-tuple-element.40.refs_2_, bf16[8,72,128]{2,1,0:T(8,128)(2,1)} %copy-done.22, bf16[8,72,128]{2,1,0:T(8,128)(2,1)} %copy-done.20, ...), custom_call_target="tpu_custom_call" | custom-call | flops 10000000000 | bytes 6000000 | tf_op jit(solution)/shard_map/first_iteration/pallas_call | solution.py:373
  102.1 3.7 %collective-permute-start.13 = (bf16[72,3200]{1,0:T(8,128)(2,1)}, bf16[72,3200]{1,0:T(8,128)(2,1)S(1)}, u32[]{:S(2)}, u32[]{:S(2)}) collective-permute-start(bf16[72,3200]{1,0:T(8,128)(2,1)} %get-tuple-element.45), channel_id=1, source_target_pairs={{32,0},{40,8},{48,16},{56,24},{57,25},{49,17},{41,9},{33,1},{34,2}... | collective-permute-start | bytes 1382408 | tf_op jit(solution)/shard_map/ppermute | solution.py:494
  105.8 10.1 %collective-permute-done.13 = bf16[72,3200]{1,0:T(8,128)(2,1)S(1)} collective-permute-done((bf16[72,3200]{1,0:T(8,128)(2,1)}, bf16[72,3200]{1,0:T(8,128)(2,1)S(1)}, u32[]{:S(2)}, u32[]{:S(2)}) %collective-permute-start.13) | collective-permute-done | bytes 460832 | tf_op jit(solution)/shard_map/ppermute | solution.py:494
  115.9 1.1 add_convert_fusion.refs_17_
  117.1 2.1 collective-permute-done.12
  119.2 1.1 add_convert_fusion.1.refs_16_
  120.4 2.8 %collective-permute-start.14 = (bf16[72,2304]{1,0:T(8,128)(2,1)S(1)}, bf16[72,2304]{1,0:T(8,128)(2,1)S(1)}, u32[]{:S(2)}, u32[]{:S(2)}) collective-permute-start(bf16[72,2304]{1,0:T(8,128)(2,1)S(1)} %get-tuple-element.101), channel_id=1, source_target_pairs={{0,8},{8,16},{16,24},{24,25},{25,17},{17,9},{9,1},{1,2},{2,10},{10... | collective-permute-start | bytes 995336 | tf_op jit(solution)/shard_map/ppermute | solution.py:499
  123.2 2.1 collective-permute-start.15
  125.3 2.5 %collective-permute-done.14.refs_18_ = bf16[72,2304]{1,0:T(8,128)(2,1)S(1)} collective-permute-done((bf16[72,2304]{1,0:T(8,128)(2,1)S(1)}, bf16[72,2304]{1,0:T(8,128)(2,1)S(1)}, u32[]{:S(2)}, u32[]{:S(2)}) %collective-permute-start.14) | collective-permute-done | bytes 331808 | tf_op jit(solution)/shard_map/ppermute | solution.py:499
  127.8 6.6 %collective-permute-done.15.refs_19_ = bf16[72,2304]{1,0:T(8,128)(2,1)S(1)} collective-permute-done((bf16[72,2304]{1,0:T(8,128)(2,1)S(1)}, bf16[72,2304]{1,0:T(8,128)(2,1)S(1)}, u32[]{:S(2)}, u32[]{:S(2)}) %collective-permute-start.15) | collective-permute-done | bytes 331808 | tf_op jit(solution)/shard_map/ppermute | solution.py:498
  135.2 37.8 %second_iteration.1 = (bf16[8,72,128]{2,1,0:T(8,128)(2,1)}, bf16[8,72,128]{2,1,0:T(8,128)(2,1)}, bf16[8,72,128]{2,1,0:T(8,128)(2,1)}, bf16[8,72,128]{2,1,0:T(8,1...) custom-call(s32[24]{0:T(128)} %stack.86.scal.refs_0_, ...), custom_call_target="tpu_custom_call" | custom-call | flops 10000000000 | bytes 6000000 | tf_op jit(solution)/shard_map/second_iteration/pallas_call | solution.py:373
  172.9 3.6 %expand.1 = (bf16[72,1024]{1,0:T(8,128)(2,1)}, bf16[72,1024]{1,0:T(8,128)(2,1)}, bf16[72,1024]{1,0:T(8,128)(2,1)}, bf16[72,1024]{1,0:T(8,128)(2,1)}) custom-call(s32[1]{0:T(128)} %get-tuple-element.39.refs_1_.count, f32[32,128]{1,0:T(8,128)} %get-tuple-element.55.posx, bf16[72,4096]{1,0:T(8,128)(2,1)} %get-tuple-element.56.found), custom_call_target="tpu_custom_call" | custom-call | tf_op jit(solution)/shard_map/expand/pallas_call | solution.py:502
  176.6 1.5 collective-permute-start.26
  178.0 2.9 %collective-permute-start.27 = (bf16[72,1024]{1,0:T(8,128)(2,1)}, bf16[72,1024]{1,0:T(8,128)(2,1)S(1)}, u32[]{:S(2)}, u32[]{:S(2)}) collective-permute-start(bf16[72,1024]{1,0:T(8,128)(2,1)} %get-tuple-element.72), channel_id=1, source_target_pairs={{0,24},{8,0},{16,8},{24,16},{1,25},{9,1},{17,9},{25,17},{2,26},{10... | collective-permute-start | bytes 442376 | tf_op jit(solution)/shard_map/ppermute | solution.py:512
  181.0 2.0 collective-permute-done.16
  183.1 2.7 %collective-permute-start.18 = (bf16[8,72,128]{2,1,0:T(8,128)(2,1)}, bf16[8,72,128]{2,1,0:T(8,128)(2,1)S(1)}, u32[]{:S(2)}, u32[]{:S(2)}) collective-permute-start(bf16[8,72,128]{2,1,0:T(8,128)(2,1)} %get-tuple-element.64), channel_id=1, source_target_pairs={{104,0},{105,1},{106,2},{107,3},{108,4},{109,5},{110,6},{111,7},{1... | collective-permute-start | bytes 442376 | tf_op jit(solution)/shard_map/ppermute | solution.py:519
  186.7 1.6 collective-permute-done.17
  188.3 2.1 collective-permute-start.19
  190.4 2.6 %collective-permute-start.20 = (bf16[8,72,128]{2,1,0:T(8,128)(2,1)}, bf16[8,72,128]{2,1,0:T(8,128)(2,1)S(1)}, u32[]{:S(2)}, u32[]{:S(2)}) collective-permute-start(bf16[8,72,128]{2,1,0:T(8,128)(2,1)} %get-tuple-element.66), channel_id=1, source_target_pairs={{112,0},{113,1},{114,2},{115,3},{116,4},{117,5},{118,6},{119,7},{1... | collective-permute-start | bytes 442376 | tf_op jit(solution)/shard_map/ppermute | solution.py:519
  193.0 2.4 %collective-permute-done.19 = bf16[8,72,128]{2,1,0:T(8,128)(2,1)S(1)} collective-permute-done((bf16[8,72,128]{2,1,0:T(8,128)(2,1)}, bf16[8,72,128]{2,1,0:T(8,128)(2,1)S(1)}, u32[]{:S(2)}, u32[]{:S(2)}) %collective-permute-start.19) | collective-permute-done | bytes 147488 | tf_op jit(solution)/shard_map/ppermute | solution.py:519
  195.4 2.9 %collective-permute-start.21 = (bf16[8,72,128]{2,1,0:T(8,128)(2,1)}, bf16[8,72,128]{2,1,0:T(8,128)(2,1)S(1)}, u32[]{:S(2)}, u32[]{:S(2)}) collective-permute-start(bf16[8,72,128]{2,1,0:T(8,128)(2,1)} %get-tuple-element.67), channel_id=1, source_target_pairs={{24,0},{25,1},{26,2},{27,3},{28,4},{29,5},{30,6},{31,7},{0,8},{1,9... | collective-permute-start | bytes 442376 | tf_op jit(solution)/shard_map/ppermute | solution.py:519
  198.3 2.4 %collective-permute-done.20 = bf16[8,72,128]{2,1,0:T(8,128)(2,1)S(1)} collective-permute-done((bf16[8,72,128]{2,1,0:T(8,128)(2,1)}, bf16[8,72,128]{2,1,0:T(8,128)(2,1)S(1)}, u32[]{:S(2)}, u32[]{:S(2)}) %collective-permute-start.20) | collective-permute-done | bytes 147488 | tf_op jit(solution)/shard_map/ppermute | solution.py:519
  200.7 3.8 %collective-permute-done.21 = bf16[8,72,128]{2,1,0:T(8,128)(2,1)S(1)} collective-permute-done((bf16[8,72,128]{2,1,0:T(8,128)(2,1)}, bf16[8,72,128]{2,1,0:T(8,128)(2,1)S(1)}, u32[]{:S(2)}, u32[]{:S(2)}) %collective-permute-start.21) | collective-permute-done | bytes 147488 | tf_op jit(solution)/shard_map/ppermute | solution.py:519
  204.5 4.6 %collective-permute-done.22 = bf16[8,72,128]{2,1,0:T(8,128)(2,1)S(1)} collective-permute-done((bf16[8,72,128]{2,1,0:T(8,128)(2,1)}, bf16[8,72,128]{2,1,0:T(8,128)(2,1)S(1)}, u32[]{:S(2)}, u32[]{:S(2)}) %collective-permute-start.22) | collective-permute-done | bytes 147488 | tf_op jit(solution)/shard_map/ppermute | solution.py:519
  209.8 2.1 collective-permute-start.23
  211.9 3.9 %collective-permute-start.24 = (bf16[8,72,32]{2,1,0:T(8,128)(2,1)S(1)}, bf16[8,72,32]{2,1,0:T(8,128)(2,1)S(1)}, u32[]{:S(2)}, u32[]{:S(2)}) collective-permute-start(bf16[8,72,32]{2,1,0:T(8,128)(2,1)S(1)} %get-tuple-element.95), channel_id=1, source_target_pairs={{1,0},{2,1},{3,2},{4,3},{5,4},{6,5},{7,6},{9,8},{10,9},{11,10},{12... | collective-permute-start | bytes 110600 | tf_op jit(solution)/shard_map/ppermute | solution.py:527
  216.8 8.2 %all-to-all-start.1 = ((bf16[72,32,32]{0,2,1:T(8,128)(2,1)}), bf16[72,32,32]{0,2,1:T(8,128)(2,1)S(1)}, u32[]{:S(2)}, u32[]{:S(2)}) async-start(bf16[72,32,32]{0,2,1:T(8,128)(2,1)} %bitcast.47), calls=%async_computation.1 | async-start | bytes 524288 | tf_op jit(solution)/shard_map/all_to_all | solution.py:515
  226.5 5.6 %all-to-all-done.1 = bf16[72,32,32]{0,2,1:T(8,128)(2,1)S(1)} async-done(((bf16[72,32,32]{0,2,1:T(8,128)(2,1)}), bf16[72,32,32]{0,2,1:T(8,128)(2,1)S(1)}, u32[]{:S(2)}, u32[]{:S(2)}) %all-to-all-start.1) | async-done | bytes 147488 | tf_op jit(solution)/shard_map/all_to_all | solution.py:515
  232.0 1.3 fusion.8
  (116 shorter events, 11.7 us)
Async XLA Ops:
  0.6 23.9 %copy-start = (bf16[4,9,128,128]{3,2,1,0:T(8,128)(2,1)S(1)}, bf16[4,9,128,128]{3,2,1,0:T(8,128)(2,1)}, u32[]{:S(2)}) copy-start(bf16[4,9,128,128]{3,2,1,0:T(8,128)(2,1)} %param.13) | copy-start | bytes 3538948
  3.4 29.4 %collective-permute-start.3 = (bf16[8,72,32]{2,1,0:T(8,128)(2,1)}, bf16[8,72,32]{2,1,0:T(8,128)(2,1)}, u32[]{:S(2)}, u32[]{:S(2)}) collective-permute-start(bf16[8,72,32]{2,1,0:T(8,128)(2,1)} %get-tuple-element.99), channel_id=1, source_target_pairs={{0,1},{1,2},{2,3},{3,4},{4,5},{5,6},{6,7},{8,9},{9,10},{10,11},{11... | collective-permute-start | bytes 110600 | tf_op jit(solution)/shard_map/ppermute | solution.py:454
  7.1 25.7 %collective-permute-start.4 = (bf16[8,72,32]{2,1,0:T(8,128)(2,1)}, bf16[8,72,32]{2,1,0:T(8,128)(2,1)}, u32[]{:S(2)}, u32[]{:S(2)}) collective-permute-start(bf16[8,72,32]{2,1,0:T(8,128)(2,1)} %get-tuple-element.98), channel_id=1, source_target_pairs={{1,0},{2,1},{3,2},{4,3},{5,4},{6,5},{7,6},{9,8},{10,9},{11,10},{12... | collective-permute-start | bytes 110600 | tf_op jit(solution)/shard_map/ppermute | solution.py:455
  15.2 25.9 %all-to-all-start = ((bf16[80,32,32]{0,2,1:T(8,128)(2,1)}), bf16[80,32,32]{0,2,1:T(8,128)(2,1)}, u32[]{:S(2)}, u32[]{:S(2)}) async-start(bf16[80,32,32]{0,2,1:T(8,128)(2,1)} %bitcast.24), calls=%async_computation | async-start | bytes 524288 | tf_op jit(solution)/shard_map/all_to_all | solution.py:475
  35.3 16.3 %collective-permute-start.10 = (bf16[8,72,128]{2,1,0:T(8,128)(2,1)}, bf16[8,72,128]{2,1,0:T(8,128)(2,1)S(1)}, u32[]{:S(2)}, u32[]{:S(2)}) collective-permute-start(bf16[8,72,128]{2,1,0:T(8,128)(2,1)} %get-tuple-element.42), channel_id=1, source_target_pairs={{0,112},{1,113},{2,114},{3,115},{4,116},{5,117},{6,118},{7,119},{8... | collective-permute-start | bytes 442376 | tf_op jit(solution)/shard_map/ppermute | solution.py:463
  41.1 13.3 %collective-permute-start.11 = (bf16[8,72,128]{2,1,0:T(8,128)(2,1)}, bf16[8,72,128]{2,1,0:T(8,128)(2,1)S(1)}, u32[]{:S(2)}, u32[]{:S(2)}) collective-permute-start(bf16[8,72,128]{2,1,0:T(8,128)(2,1)} %get-tuple-element.43), channel_id=1, source_target_pairs={{0,120},{1,121},{2,122},{3,123},{4,124},{5,125},{6,126},{7,127},{8... | collective-permute-start | bytes 442376 | tf_op jit(solution)/shard_map/ppermute | solution.py:463
  42.2 9.4 %copy-start.6 = (bf16[80,1024]{1,0:T(8,128)(2,1)}, bf16[80,1024]{1,0:T(8,128)(2,1)S(1)}, u32[]{:S(2)}) copy-start(bf16[80,1024]{1,0:T(8,128)(2,1)S(1)} %copy.34.pay0) | copy-start | bytes 491524
  42.2 12.3 %collective-permute-start = (bf16[80,1024]{1,0:T(8,128)(2,1)S(1)}, bf16[80,1024]{1,0:T(8,128)(2,1)S(1)}, u32[]{:S(2)}, u32[]{:S(2)}) collective-permute-start(bf16[80,1024]{1,0:T(8,128)(2,1)S(1)} %copy.34.pay0), channel_id=1, source_target_pairs={{0,8},{8,16},{16,24},{24,0},{1,9},{9,17},{17,25},{25,1},{2,10},{10... | collective-permute-start | bytes 491528 | tf_op jit(solution)/shard_map/ppermute | solution.py:476
  43.2 11.9 %collective-permute-start.1 = (bf16[80,1024]{1,0:T(8,128)(2,1)S(1)}, bf16[80,1024]{1,0:T(8,128)(2,1)S(1)}, u32[]{:S(2)}, u32[]{:S(2)}) collective-permute-start(bf16[80,1024]{1,0:T(8,128)(2,1)S(1)} %copy.34.pay0), channel_id=1, source_target_pairs={{0,16},{8,24},{16,0},{24,8},{1,17},{9,25},{17,1},{25,9},{2,18},{10... | collective-permute-start | bytes 491528 | tf_op jit(solution)/shard_map/ppermute | solution.py:476
  43.2 15.4 %collective-permute-start.2 = (bf16[80,1024]{1,0:T(8,128)(2,1)S(1)}, bf16[80,1024]{1,0:T(8,128)(2,1)S(1)}, u32[]{:S(2)}, u32[]{:S(2)}) collective-permute-start(bf16[80,1024]{1,0:T(8,128)(2,1)S(1)} %copy.34.pay0), channel_id=1, source_target_pairs={{0,24},{8,0},{16,8},{24,16},{1,25},{9,1},{17,9},{25,17},{2,26},{10... | collective-permute-start | bytes 491528 | tf_op jit(solution)/shard_map/ppermute | solution.py:476
  46.2 5.4 %copy-start.12 = (bf16[69,128]{1,0:T(8,128)(2,1)S(1)}, bf16[69,128]{1,0:T(8,128)(2,1)}, u32[]{:S(2)}) copy-start(bf16[69,128]{1,0:T(8,128)(2,1)} %param.14) | copy-start | bytes 52996
  46.2 5.4 %copy-start.13 = (bf16[128,69]{0,1:T(8,128)(2,1)S(1)}, bf16[128,69]{0,1:T(8,128)(2,1)}, u32[]{:S(2)}) copy-start(bf16[128,69]{0,1:T(8,128)(2,1)} %param.12) | copy-start | bytes 52996
  46.2 5.5 %copy-start.27 = (bf16[8,72,128]{2,1,0:T(8,128)(2,1)S(1)}, bf16[8,72,128]{2,1,0:T(8,128)(2,1)}, u32[]{:S(2)}) copy-start(bf16[8,72,128]{2,1,0:T(8,128)(2,1)} %get-tuple-element.42) | copy-start | bytes 442372
  46.2 8.2 %copy-start.26 = (bf16[8,72,128]{2,1,0:T(8,128)(2,1)S(1)}, bf16[8,72,128]{2,1,0:T(8,128)(2,1)}, u32[]{:S(2)}) copy-start(bf16[8,72,128]{2,1,0:T(8,128)(2,1)} %get-tuple-element.43) | copy-start | bytes 442372
  46.2 8.3 %copy-start.25 = (bf16[8,72,128]{2,1,0:T(8,128)(2,1)S(1)}, bf16[8,72,128]{2,1,0:T(8,128)(2,1)}, u32[]{:S(2)}) copy-start(bf16[8,72,128]{2,1,0:T(8,128)(2,1)} %get-tuple-element.41) | copy-start | bytes 442372
  46.2 12.3 %copy-start.17 = (bf16[8,72,128]{2,1,0:T(8,128)(2,1)S(1)}, bf16[8,72,128]{2,1,0:T(8,128)(2,1)}, u32[]{:S(2)}) copy-start(bf16[8,72,128]{2,1,0:T(8,128)(2,1)} %get-tuple-element.40.refs_2_) | copy-start | bytes 442372
  51.7 13.9 %copy-start.18 = (bf16[8,72,128]{2,1,0:T(8,128)(2,1)}, bf16[8,72,128]{2,1,0:T(8,128)(2,1)S(1)}, u32[]{:S(2)}) copy-start(bf16[8,72,128]{2,1,0:T(8,128)(2,1)S(1)} %collective-permute-done.10.refs_8_) | copy-start | bytes 442372
  51.7 12.4 %collective-permute-start.6 = (bf16[8,72,128]{2,1,0:T(8,128)(2,1)S(1)}, bf16[8,72,128]{2,1,0:T(8,128)(2,1)S(1)}, u32[]{:S(2)}, u32[]{:S(2)}) collective-permute-start(bf16[8,72,128]{2,1,0:T(8,128)(2,1)S(1)} %copy-done.27), channel_id=1, source_target_pairs={{0,16},{1,17},{2,18},{3,19},{4,20},{5,21},{6,22},{7,23},{8,24},{9,... | collective-permute-start | bytes 442376 | tf_op jit(solution)/shard_map/ppermute | solution.py:463
  54.4 11.2 %copy-start.19 = (bf16[8,72,128]{2,1,0:T(8,128)(2,1)}, bf16[8,72,128]{2,1,0:T(8,128)(2,1)S(1)}, u32[]{:S(2)}) copy-start(bf16[8,72,128]{2,1,0:T(8,128)(2,1)S(1)} %collective-permute-done.11.refs_9_) | copy-start | bytes 442372
  54.4 9.7 %collective-permute-start.7 = (bf16[8,72,128]{2,1,0:T(8,128)(2,1)S(1)}, bf16[8,72,128]{2,1,0:T(8,128)(2,1)S(1)}, u32[]{:S(2)}, u32[]{:S(2)}) collective-permute-start(bf16[8,72,128]{2,1,0:T(8,128)(2,1)S(1)} %copy-done.26), channel_id=1, source_target_pairs={{0,24},{1,25},{2,26},{3,27},{4,28},{5,29},{6,30},{7,31},{8,0},{9,1... | collective-permute-start | bytes 442376 | tf_op jit(solution)/shard_map/ppermute | solution.py:463
  54.5 5.4 %copy-start.7 = (bf16[80,1024]{1,0:T(8,128)(2,1)}, bf16[80,1024]{1,0:T(8,128)(2,1)S(1)}, u32[]{:S(2)}) copy-start(bf16[80,1024]{1,0:T(8,128)(2,1)S(1)} %collective-permute-done.pay1) | copy-start | bytes 491524
  54.5 9.5 %collective-permute-start.5 = (bf16[8,72,128]{2,1,0:T(8,128)(2,1)S(1)}, bf16[8,72,128]{2,1,0:T(8,128)(2,1)S(1)}, u32[]{:S(2)}, u32[]{:S(2)}) collective-permute-start(bf16[8,72,128]{2,1,0:T(8,128)(2,1)S(1)} %copy-done.25), channel_id=1, source_target_pairs={{0,8},{1,9},{2,10},{3,11},{4,12},{5,13},{6,14},{7,15},{8,16},{9,17... | collective-permute-start | bytes 442376 | tf_op jit(solution)/shard_map/ppermute | solution.py:463
  55.0 10.5 %collective-permute-start.9 = (bf16[8,72,128]{2,1,0:T(8,128)(2,1)S(1)}, bf16[8,72,128]{2,1,0:T(8,128)(2,1)S(1)}, u32[]{:S(2)}, u32[]{:S(2)}) collective-permute-start(bf16[8,72,128]{2,1,0:T(8,128)(2,1)S(1)} %copy-done.25), channel_id=1, source_target_pairs={{0,104},{1,105},{2,106},{3,107},{4,108},{5,109},{6,110},{7,111},{8... | collective-permute-start | bytes 442376 | tf_op jit(solution)/shard_map/ppermute | solution.py:463
  58.5 7.0 %collective-permute-start.8 = (bf16[8,72,128]{2,1,0:T(8,128)(2,1)S(1)}, bf16[8,72,128]{2,1,0:T(8,128)(2,1)S(1)}, u32[]{:S(2)}, u32[]{:S(2)}) collective-permute-start(bf16[8,72,128]{2,1,0:T(8,128)(2,1)S(1)} %copy-done.17), channel_id=1, source_target_pairs={{0,96},{1,97},{2,98},{3,99},{4,100},{5,101},{6,102},{7,103},{8,104... | collective-permute-start | bytes 442376 | tf_op jit(solution)/shard_map/ppermute | solution.py:463
  102.1 13.8 %collective-permute-start.13 = (bf16[72,3200]{1,0:T(8,128)(2,1)}, bf16[72,3200]{1,0:T(8,128)(2,1)S(1)}, u32[]{:S(2)}, u32[]{:S(2)}) collective-permute-start(bf16[72,3200]{1,0:T(8,128)(2,1)} %get-tuple-element.45), channel_id=1, source_target_pairs={{32,0},{40,8},{48,16},{56,24},{57,25},{49,17},{41,9},{33,1},{34,2}... | collective-permute-start | bytes 1382408 | tf_op jit(solution)/shard_map/ppermute | solution.py:494
  105.8 13.4 %collective-permute-start.12 = (bf16[72,3200]{1,0:T(8,128)(2,1)}, bf16[72,3200]{1,0:T(8,128)(2,1)S(1)}, u32[]{:S(2)}, u32[]{:S(2)}) collective-permute-start(bf16[72,3200]{1,0:T(8,128)(2,1)} %get-tuple-element.46), channel_id=1, source_target_pairs={{0,32},{8,40},{16,48},{24,56},{25,57},{17,49},{9,41},{1,33},{2,34}... | collective-permute-start | bytes 1382408 | tf_op jit(solution)/shard_map/ppermute | solution.py:493
  117.0 17.4 %copy-start.4 = (bf16[72,3200]{1,0:T(8,128)(2,1)}, bf16[72,3200]{1,0:T(8,128)(2,1)S(1)}, u32[]{:S(2)}) copy-start(bf16[72,3200]{1,0:T(8,128)(2,1)S(1)} %add_convert_fusion.refs_17_) | copy-start | bytes 1382404
  120.3 14.1 %copy-start.5 = (bf16[72,3200]{1,0:T(8,128)(2,1)}, bf16[72,3200]{1,0:T(8,128)(2,1)S(1)}, u32[]{:S(2)}) copy-start(bf16[72,3200]{1,0:T(8,128)(2,1)S(1)} %add_convert_fusion.1.refs_16_) | copy-start | bytes 1382404
  120.4 7.4 %collective-permute-start.14 = (bf16[72,2304]{1,0:T(8,128)(2,1)S(1)}, bf16[72,2304]{1,0:T(8,128)(2,1)S(1)}, u32[]{:S(2)}, u32[]{:S(2)}) collective-permute-start(bf16[72,2304]{1,0:T(8,128)(2,1)S(1)} %get-tuple-element.101), channel_id=1, source_target_pairs={{0,8},{8,16},{16,24},{24,25},{25,17},{17,9},{9,1},{1,2},{2,10},{10... | collective-permute-start | bytes 995336 | tf_op jit(solution)/shard_map/ppermute | solution.py:499
  123.2 11.2 %collective-permute-start.15 = (bf16[72,2304]{1,0:T(8,128)(2,1)S(1)}, bf16[72,2304]{1,0:T(8,128)(2,1)S(1)}, u32[]{:S(2)}, u32[]{:S(2)}) collective-permute-start(bf16[72,2304]{1,0:T(8,128)(2,1)S(1)} %get-tuple-element.100), channel_id=1, source_target_pairs={{8,0},{16,8},{24,16},{25,24},{17,25},{9,17},{1,9},{2,1},{10,2},{18... | collective-permute-start | bytes 995336 | tf_op jit(solution)/shard_map/ppermute | solution.py:498
  127.8 6.6 %copy-start.15 = (bf16[72,2304]{1,0:T(8,128)(2,1)}, bf16[72,2304]{1,0:T(8,128)(2,1)S(1)}, u32[]{:S(2)}) copy-start(bf16[72,2304]{1,0:T(8,128)(2,1)S(1)} %collective-permute-done.14.refs_18_) | copy-start | bytes 995332
  176.5 6.6 %collective-permute-start.16 = (bf16[8,72,128]{2,1,0:T(8,128)(2,1)}, bf16[8,72,128]{2,1,0:T(8,128)(2,1)S(1)}, u32[]{:S(2)}, u32[]{:S(2)}) collective-permute-start(bf16[8,72,128]{2,1,0:T(8,128)(2,1)} %get-tuple-element.62), channel_id=1, source_target_pairs={{96,0},{97,1},{98,2},{99,3},{100,4},{101,5},{102,6},{103,7},{104,8... | collective-permute-start | bytes 442376 | tf_op jit(solution)/shard_map/ppermute | solution.py:519
  176.5 39.3 %collective-permute-start.25 = (bf16[72,1024]{1,0:T(8,128)(2,1)}, bf16[72,1024]{1,0:T(8,128)(2,1)S(1)}, u32[]{:S(2)}, u32[]{:S(2)}) collective-permute-start(bf16[72,1024]{1,0:T(8,128)(2,1)} %get-tuple-element.70), channel_id=1, source_target_pairs={{0,8},{8,16},{16,24},{24,0},{1,9},{9,17},{17,25},{25,1},{2,10},{10... | collective-permute-start | bytes 442376 | tf_op jit(solution)/shard_map/ppermute | solution.py:512
  176.6 39.2 %collective-permute-start.26 = (bf16[72,1024]{1,0:T(8,128)(2,1)}, bf16[72,1024]{1,0:T(8,128)(2,1)S(1)}, u32[]{:S(2)}, u32[]{:S(2)}) collective-permute-start(bf16[72,1024]{1,0:T(8,128)(2,1)} %get-tuple-element.71), channel_id=1, source_target_pairs={{0,16},{8,24},{16,0},{24,8},{1,17},{9,25},{17,1},{25,9},{2,18},{10... | collective-permute-start | bytes 442376 | tf_op jit(solution)/shard_map/ppermute | solution.py:512
  178.0 37.8 %collective-permute-start.27 = (bf16[72,1024]{1,0:T(8,128)(2,1)}, bf16[72,1024]{1,0:T(8,128)(2,1)S(1)}, u32[]{:S(2)}, u32[]{:S(2)}) collective-permute-start(bf16[72,1024]{1,0:T(8,128)(2,1)} %get-tuple-element.72), channel_id=1, source_target_pairs={{0,24},{8,0},{16,8},{24,16},{1,25},{9,1},{17,9},{25,17},{2,26},{10... | collective-permute-start | bytes 442376 | tf_op jit(solution)/shard_map/ppermute | solution.py:512
  181.0 7.3 %collective-permute-start.17 = (bf16[8,72,128]{2,1,0:T(8,128)(2,1)}, bf16[8,72,128]{2,1,0:T(8,128)(2,1)S(1)}, u32[]{:S(2)}, u32[]{:S(2)}) collective-permute-start(bf16[8,72,128]{2,1,0:T(8,128)(2,1)} %get-tuple-element.63), channel_id=1, source_target_pairs={{8,0},{9,1},{10,2},{11,3},{12,4},{13,5},{14,6},{15,7},{16,8},{17,9... | collective-permute-start | bytes 442376 | tf_op jit(solution)/shard_map/ppermute | solution.py:519
  183.1 7.4 %collective-permute-start.18 = (bf16[8,72,128]{2,1,0:T(8,128)(2,1)}, bf16[8,72,128]{2,1,0:T(8,128)(2,1)S(1)}, u32[]{:S(2)}, u32[]{:S(2)}) collective-permute-start(bf16[8,72,128]{2,1,0:T(8,128)(2,1)} %get-tuple-element.64), channel_id=1, source_target_pairs={{104,0},{105,1},{106,2},{107,3},{108,4},{109,5},{110,6},{111,7},{1... | collective-permute-start | bytes 442376 | tf_op jit(solution)/shard_map/ppermute | solution.py:519
  188.3 7.1 %collective-permute-start.19 = (bf16[8,72,128]{2,1,0:T(8,128)(2,1)}, bf16[8,72,128]{2,1,0:T(8,128)(2,1)S(1)}, u32[]{:S(2)}, u32[]{:S(2)}) collective-permute-start(bf16[8,72,128]{2,1,0:T(8,128)(2,1)} %get-tuple-element.65), channel_id=1, source_target_pairs={{16,0},{17,1},{18,2},{19,3},{20,4},{21,5},{22,6},{23,7},{24,8},{25... | collective-permute-start | bytes 442376 | tf_op jit(solution)/shard_map/ppermute | solution.py:519
  190.4 10.2 %collective-permute-start.20 = (bf16[8,72,128]{2,1,0:T(8,128)(2,1)}, bf16[8,72,128]{2,1,0:T(8,128)(2,1)S(1)}, u32[]{:S(2)}, u32[]{:S(2)}) collective-permute-start(bf16[8,72,128]{2,1,0:T(8,128)(2,1)} %get-tuple-element.66), channel_id=1, source_target_pairs={{112,0},{113,1},{114,2},{115,3},{116,4},{117,5},{118,6},{119,7},{1... | collective-permute-start | bytes 442376 | tf_op jit(solution)/shard_map/ppermute | solution.py:519
  195.4 9.1 %collective-permute-start.21 = (bf16[8,72,128]{2,1,0:T(8,128)(2,1)}, bf16[8,72,128]{2,1,0:T(8,128)(2,1)S(1)}, u32[]{:S(2)}, u32[]{:S(2)}) collective-permute-start(bf16[8,72,128]{2,1,0:T(8,128)(2,1)} %get-tuple-element.67), channel_id=1, source_target_pairs={{24,0},{25,1},{26,2},{27,3},{28,4},{29,5},{30,6},{31,7},{0,8},{1,9... | collective-permute-start | bytes 442376 | tf_op jit(solution)/shard_map/ppermute | solution.py:519
  200.7 8.4 %collective-permute-start.22 = (bf16[8,72,128]{2,1,0:T(8,128)(2,1)}, bf16[8,72,128]{2,1,0:T(8,128)(2,1)S(1)}, u32[]{:S(2)}, u32[]{:S(2)}) collective-permute-start(bf16[8,72,128]{2,1,0:T(8,128)(2,1)} %get-tuple-element.68), channel_id=1, source_target_pairs={{120,0},{121,1},{122,2},{123,3},{124,4},{125,5},{126,6},{127,7},{9... | collective-permute-start | bytes 442376 | tf_op jit(solution)/shard_map/ppermute | solution.py:519
  209.2 6.7 %copy-start.11 = (bf16[72,1024]{1,0:T(8,128)(2,1)S(1)}, bf16[72,1024]{1,0:T(8,128)(2,1)}, u32[]{:S(2)}) copy-start(bf16[72,1024]{1,0:T(8,128)(2,1)} %get-tuple-element.69) | copy-start | bytes 442372
  209.3 15.9 %copy-start.3 = (f32[69,8,256]{2,1,0:T(8,128)S(1)}, f32[69,8,256]{2,1,0:T(8,128)}, u32[]{:S(2)}) copy-start(f32[69,8,256]{2,1,0:T(8,128)} %param.11) | copy-start | bytes 1695748
  209.8 22.2 %copy-start.10 = (f32[69,512]{1,0:T(8,128)S(1)}, f32[69,512]{1,0:T(8,128)}, u32[]{:S(2)}) copy-start(f32[69,512]{1,0:T(8,128)} %values.1) | copy-start | bytes 423940
  209.8 22.2 %copy-start.28 = (s32[1,512]{1,0:T(1,128)S(1)}, s32[1,512]{1,0:T(1,128)}, u32[]{:S(2)}) copy-start(s32[1,512]{1,0:T(1,128)} %get-tuple-element.73) | copy-start | bytes 6148
  209.8 15.4 %collective-permute-start.23 = (bf16[8,72,32]{2,1,0:T(8,128)(2,1)S(1)}, bf16[8,72,32]{2,1,0:T(8,128)(2,1)S(1)}, u32[]{:S(2)}, u32[]{:S(2)}) collective-permute-start(bf16[8,72,32]{2,1,0:T(8,128)(2,1)S(1)} %get-tuple-element.94), channel_id=1, source_target_pairs={{0,1},{1,2},{2,3},{3,4},{4,5},{5,6},{6,7},{8,9},{9,10},{10,11},{11... | collective-permute-start | bytes 110600 | tf_op jit(solution)/shard_map/ppermute | solution.py:526
  211.9 13.3 %collective-permute-start.24 = (bf16[8,72,32]{2,1,0:T(8,128)(2,1)S(1)}, bf16[8,72,32]{2,1,0:T(8,128)(2,1)S(1)}, u32[]{:S(2)}, u32[]{:S(2)}) collective-permute-start(bf16[8,72,32]{2,1,0:T(8,128)(2,1)S(1)} %get-tuple-element.95), channel_id=1, source_target_pairs={{1,0},{2,1},{3,2},{4,3},{5,4},{6,5},{7,6},{9,8},{10,9},{11,10},{12... | collective-permute-start | bytes 110600 | tf_op jit(solution)/shard_map/ppermute | solution.py:527
  216.8 15.2 %all-to-all-start.1 = ((bf16[72,32,32]{0,2,1:T(8,128)(2,1)}), bf16[72,32,32]{0,2,1:T(8,128)(2,1)S(1)}, u32[]{:S(2)}, u32[]{:S(2)}) async-start(bf16[72,32,32]{0,2,1:T(8,128)(2,1)} %bitcast.47), calls=%async_computation.1 | async-start | bytes 524288 | tf_op jit(solution)/shard_map/all_to_all | solution.py:515
  (11 other events, 20.3 us)

commit v2 on v1

--- a/solution.py
+++ b/solution.py
@@ -42,17 +42,11 @@
 
 
 def family(m):
-    pairs = []
-    for y in range(4):
-        for s in range(4):
-            to = y if m < 4 else (y + (1 if s >= 2 else -1)) % 4
-            for l in range(8):
-                pairs.append((device(4 * y + s, l), device(4 * to + (s + m) % 4, l)))
-    return pairs
-
-
-def turn(m):
     return [(g[s], g[(s + m) % 4]) for g in GROUPS_4 for s in range(4)]
+
+
+def swap(x):
+    return [(g[s], g[s ^ x]) for g in GROUPS_4 for s in range(4)]
 
 
 def nt(a, b):
@@ -111,6 +105,25 @@
                     outs[m][r] = x
 
 
+def order_kernel(scal, *refs):
+    chunks, outs = refs[0:4], refs[4:6]
+    for m in range(4):
+        for c in range(4):
+            @pl.when(scal[8 + m] == c)
+            def _():
+                outs[c // 2][8 * (c % 2) : 8 * (c % 2) + 8] = chunks[m][...]
+
+
+def gather_kernel(scal, low, low_in, high, high_in, *outs):
+    for m in range(4):
+        for c in range(4):
+            @pl.when(scal[8 + m] == c)
+            def _():
+                rows = pl.ds(8 * (c % 2), 8)
+                x, y = (low, low_in) if c < 2 else (high, high_in)
+                outs[m][...] = (x[rows].astype(F32) + y[rows].astype(F32)).astype(BF)
+
+
 def compact_kernel(scal, pay0, pay1, pay2, pay3, comp, posx, count, total):
     pays = (pay0, pay1, pay2, pay3)
     k64 = scal[6].astype(F32)
@@ -132,9 +145,7 @@
     offset = nn(jnp.where(col4 < row4, 1.0, 0.0).astype(BF), sums.astype(BF))
     place = before + offset
     owned = jnp.where(own > 0.0, place, -1.0)
-    for m in range(4):
-        to = 8 * ((4 - m) % 4)
-        posx[to : to + 8, :] = owned[8 * m : 8 * m + 8]
+    posx[...] = owned
     total[...] = jnp.where(mine > 0.0, place, -1.0)
     number = jnp.sum(mine).astype(jnp.int32)
     count[0] = number
@@ -190,13 +201,13 @@
 
 def iterate(second, *refs):
     scal, count = refs[0:2]
-    chunks = refs[2:10]
-    enc_eye, dec_eye, dec_n, wf, wb, comp = refs[10:16]
-    refs = refs[16:]
+    chunks = refs[2:6]
+    enc_eye, dec_eye, dec_n, wf, wb, comp = refs[6:12]
+    refs = refs[12:]
     if second:
         tots, from_prev, from_next = refs[0:2], refs[2], refs[3]
-        outs, found = refs[4:12], refs[12]
-        refs = refs[13:]
+        outs, found = refs[4:8], refs[8]
+        refs = refs[9:]
     else:
         outs = refs[0:2]
         refs = refs[2:]
@@ -204,12 +215,14 @@
 
     act[60:96] = jnp.zeros((36, 96, 384), BF)
 
-    for f in range(8):
-        base = 8 * scal[8 + f]
-        for r in range(8):
-            both = tn(chunks[f][r], enc_eye[...])
-            h[base + r + OFF] = both[:, 0:128]
-            st[base + r] = both[16:112, 128:256]
+    for i in range(64):
+        chunk = chunks[i // 16][i % 16]
+        if 16 <= i < 48:
+            both = tn(chunk, enc_eye[...])
+            st[i - 16] = both[16:112, 128:256]
+        else:
+            both = tn(chunk, enc_eye[:, 0:128])
+        h[i + OFF] = both[:, 0:128]
     if second:
         for half in range(2):
             tot = tots[half]
@@ -225,7 +238,7 @@
                     both = tn(add.astype(BF), enc_eye[...]).reshape(16, 32, 256)
                     h[row + OFF : row + OFF + 16, 16 + 32 * sec : 48 + 32 * sec, :] -= STEP * both[:, :, 0:128]
                     if half + c == 1:
-                        st[row : row + 16, 32 * sec : 32 + 32 * sec, :] -= STEP * both[:, :, 128:256]
+                        st[row - 16 : row, 32 * sec : 32 + 32 * sec, :] -= STEP * both[:, :, 128:256]
                         ga[row - 16 : row, 32 * sec : 32 * sec + 32, :] = 0.75 * both[:, :, 128:256]
             low = tn(from_prev[:, 2048 + 128 * half : 2176 + 128 * half], enc_eye[:, 0:128])
             high = tn(from_next[:, 2048 + 128 * half : 2176 + 128 * half], enc_eye[:, 0:128])
@@ -263,7 +276,7 @@
 
     for c in range(4):
         a = h[16 + OFF + 8 * c : 24 + OFF + 8 * c, 16:112, :].reshape(768, 128).astype(BF)
-        b = st[16 + 8 * c : 24 + 8 * c].reshape(768, 128).astype(BF)
+        b = st[8 * c : 8 + 8 * c].reshape(768, 128).astype(BF)
         fct[:, 768 * c : 768 * c + 768] = nt(dec_eye[...], jnp.concatenate([a, b], axis=1)).astype(BF)
 
     g[...] = jnp.zeros_like(g)
@@ -324,18 +337,16 @@
     if second:
         ga[:, 0:16, :] = jnp.zeros((32, 16, 128), F32)
         ga[:, 80:96, :] = jnp.zeros((32, 16, 128), F32)
-        for f in range(8):
-            base = 8 * scal[8 + f]
-            inside = (base >= 16) & (base < 48)
-            grow = jnp.where(inside, base - 16, 0)
-            keep = jnp.where(inside, 1.0, 0.0)
-            for r in range(8):
-                x = bk[base + r + OFF, 8:104, :].astype(BF)
-                y = (keep * (g[grow + r] + ga[grow + r])).astype(BF)
-                x = jnp.concatenate([x, y], axis=1)
-                edge = jnp.zeros((16, 256), BF)
-                x = jnp.concatenate([edge, x, edge], axis=0)
-                outs[f][r] = (-STEP * nt(enc_eye[...], x)).astype(BF)
+        edge = jnp.zeros((16, 128), BF)
+        for i in range(64):
+            x = jnp.concatenate([edge, bk[i + OFF, 8:104, :].astype(BF), edge], axis=0)
+            if 16 <= i < 48:
+                y = (g[i - 16] + ga[i - 16]).astype(BF)
+                y = jnp.concatenate([edge, y, edge], axis=0)
+                val = nt(enc_eye[...], jnp.concatenate([x, y], axis=1))
+            else:
+                val = nt(enc_eye[:, 0:128], x)
+            outs[i // 16][i % 16] = (-STEP * val).astype(BF)
     else:
         for half in range(2):
             for c in range(2):
@@ -367,7 +378,7 @@
     smem = pl.BlockSpec(memory_space=pltpu.SMEM)
     vmem = pl.BlockSpec(memory_space=pltpu.VMEM)
     if second:
-        shapes = [jax.ShapeDtypeStruct((8, V, 128), BF)] * 8 + [jax.ShapeDtypeStruct((V, 4096), BF)]
+        shapes = [jax.ShapeDtypeStruct((16, V, 128), BF)] * 4 + [jax.ShapeDtypeStruct((V, 4096), BF)]
     else:
         shapes = [jax.ShapeDtypeStruct((V, 3200), BF)] * 2
     return pl.pallas_call(
@@ -376,7 +387,7 @@
         in_specs=[smem, smem] + [vmem] * len(arrays),
         out_specs=[vmem] * len(shapes),
         scratch_shapes=[
-            pltpu.VMEM((64, 96, 128), F32),
+            pltpu.VMEM((32, 96, 128), F32),
             pltpu.VMEM((ROWS, 128, 128), F32),
             pltpu.VMEM((ROWS, 96, 384), BF),
             pltpu.VMEM((4, ROWS, 96, 128), BF),
@@ -441,7 +452,7 @@
     k = block_of(sub)
     top = 256 * lat + 64 * k
     came = [(sub - m) % 4 for m in range(4)]
-    tables = [c + 2 for c in came] + [jnp.where(c >= 2, c - 2, c + 6) for c in came]
+    tables = came + [jnp.int32(0)] * 4
     d = dilations
     scal = jnp.stack(
         [d[0], d[1], d[2], d[3], 32 - top, 2048 + 32 - top, 64 * k, jnp.int32(0)]
@@ -460,7 +471,15 @@
         out_specs=[vmem] * 4,
         name="split",
     )(scal, cells, before, after)
-    chunks = [sends[0]] + [lax.ppermute(sends[m % 4], AXES, family(m)) for m in range(1, 8)]
+    chunks = [sends[0]] + [lax.ppermute(sends[m], AXES, family(m)) for m in range(1, 4)]
+    low, high = pl.pallas_call(
+        order_kernel,
+        out_shape=[jax.ShapeDtypeStruct((16, V, 128), BF)] * 2,
+        in_specs=[smem] + [vmem] * 4,
+        out_specs=[vmem] * 2,
+        name="order",
+    )(scal, *chunks)
+    chunks = [lax.ppermute(high, AXES, LON_UP), low, high, lax.ppermute(low, AXES, LON_DOWN)]
 
     rows = obs_dest.shape[0]
     alive = (jnp.arange(rows, dtype=jnp.int32) < obs_count[0]).astype(F32)
@@ -473,7 +492,8 @@
     )(obs_values, (alive * obs_prec)[None, :], obs_frac, obs_dest.reshape(1, rows), obs_cell[None, :])
     pick = (slots.reshape(rows, 1) == jnp.arange(1024, dtype=jnp.int32)[None, :]).astype(BF)
     arrived = lax.all_to_all(packed, AXES, split_axis=1, concat_axis=1, tiled=True, axis_index_groups=GROUPS_32)
-    others = [lax.ppermute(arrived, AXES, turn(m)) for m in range(1, 4)]
+    across = lax.ppermute(arrived, AXES, swap(2))
+    others = [lax.ppermute(arrived, AXES, swap(1)), across, lax.ppermute(across, AXES, swap(1))]
     comp, posx, count = pl.pallas_call(
         compact_kernel,
         out_shape=[
@@ -499,6 +519,9 @@
     from_prev = lax.ppermute(jnp.concatenate([left[:, 2048:3072], right[:, 2048:3072]] + extra, axis=1), AXES, LAT_UP)
     *moves, found = iteration(True, scal, count, *chunks, *weights, comp, left, right, from_prev, from_next)
 
+    low_in = lax.ppermute(moves[3], AXES, LON_UP)
+    high_in = lax.ppermute(moves[0], AXES, LON_DOWN)
+
     spread = pl.pallas_call(
         expand_kernel,
         out_shape=[jax.ShapeDtypeStruct((V, 1024), BF)] * 4,
@@ -507,18 +530,23 @@
         scratch_shapes=[pltpu.VMEM((V, 4096), F32)],
         name="expand",
     )(count, posx, found)
-    moves = lax.optimization_barrier((*moves, *spread))
-    moves, spread = moves[0:8], moves[8:12]
-    parts = [lax.ppermute(spread[m], AXES, turn(m)) for m in range(1, 4)]
+    parts = [lax.ppermute(spread[m], AXES, swap(m)) for m in range(1, 4)]
     parts = [p.astype(F32) for p in [spread[0]] + parts]
     spread = (parts[0] + parts[1] + parts[2] + parts[3]).astype(BF)
     spread = lax.all_to_all(spread, AXES, split_axis=1, concat_axis=1, tiled=True, axis_index_groups=GROUPS_32)
     equivalent = jnp.einsum("vs,rs->vr", spread[0:69], pick, preferred_element_type=F32)
     innovation = alive[None, :] * (equivalent - obs_values)
 
-    back = [moves[0]] + [lax.ppermute(moves[m], AXES, [(b, a) for a, b in family(m)]) for m in range(1, 8)]
+    moves = pl.pallas_call(
+        gather_kernel,
+        out_shape=[jax.ShapeDtypeStruct((8, V, 128), BF)] * 4,
+        in_specs=[smem] + [vmem] * 4,
+        out_specs=[vmem] * 4,
+        name="gather",
+    )(scal, moves[1], low_in, moves[2], high_in)
+    back = [moves[0]] + [lax.ppermute(moves[m], AXES, [(b, a) for a, b in family(m)]) for m in range(1, 4)]
     total = jnp.zeros((8, V, 320), F32)
-    summed = jnp.stack([back[m].astype(F32) + back[m + 4].astype(F32) for m in range(4)])
+    summed = jnp.stack(back).astype(F32)
     for b in range(4):
         m = (jnp.where(flip, 3 - b, b) - sub) % 4
         block = lax.dynamic_index_in_dim(summed, m, 0, keepdims=False)

time: 237 us -> 217 us (0.916)
  waiting for transfers between devices: 45.1 us -> 27.8 us
  starting transfers between devices: 69.3 us -> 55.5 us
  Pallas kernels: 86 us -> 93.7 us
  local copies, waits for them, and re-layouts: 13.8 us -> 16.5 us
    ppermute x7 -> x3, waiting for transfers between devices: 16.7 us -> 0.01 us  [on_device(): lax.ppermute(moves[m], AXES, [(b, a) for a, b in family(m)])]
    ppermute x7 -> x3, starting transfers between devices: 10.3 us -> 3.42 us  [on_device(): lax.ppermute(moves[m], AXES, [(b, a) for a, b in family(m)])]
    ppermute x1, waiting for transfers between devices: 0.01 us -> 5.81 us  [on_device(): edge_down = lax.ppermute(total[:, :, 0:32].astype(BF), AXES, BAND_DOWN)]
    all_to_all x1, waiting for transfers between devices: 5.56 us -> 0.01 us  [on_device(): lax.all_to_all(spread, AXES, split_axis=1, concat_axis=1, tiled=True, axi...]
    pallas_call x0 -> x2, Pallas kernels: none -> 4.42 us  [the longest x1 2.29 us: on_device(): pl.pallas_call(gather_kernel, out_shape=[jax.ShapeDtypeStruct((8, V, 128)...]
    ppermute x13, starting transfers between devices: 21 us -> 17.3 us  [the longest x3 6.55 us: on_device(): lax.ppermute(sends[m], AXES, family(m))]
    pallas_call x2, Pallas kernels: 73.5 us -> 76.9 us  [iteration(): pl.pallas_call(functools.partial(iterate, second), out_shape=shapes, in_s...]
    unnamed x60 -> x50, local copies, waits for them, and re-layouts: 3.97 us -> 6.86 us
  transfers between devices with their start and end apart: 30 -> 26, of which waited for: 12 -> 7; matrix products, arithmetic and copies ran while one was open for 9% -> 10% of each run, Pallas kernels for 4% -> 8%
where the time goes in v2:
time: 217 us; the launch traced here: 213 us
  Pallas kernels  93.7 us (43%)
  starting transfers between devices  55.5 us (26%)
  waiting for transfers between devices  27.8 us (13%)
  local copies, waits for them, and re-layouts  16.5 us (8%)
  other arithmetic  13.5 us (6%)
  between operations  4.88 us (2%)
    pallas_call x2, Pallas kernels, iteration(): pl.pallas_call(functools.partial(iterate, second), out_shape=shapes, in_s...  76.9 us
    ppermute x1, waiting for transfers between devices, on_device(): right_in = lax.ppermute(left, AXES, LON_DOWN)  10.2 us
    all_to_all x1, starting transfers between devices, on_device(): lax.all_to_all(packed, AXES, split_axis=1, concat_axis=1, tiled=True, axi...  9.37 us
    unnamed x50, local copies, waits for them, and re-layouts  6.86 us
    ppermute x1, waiting for transfers between devices, on_device(): lax.ppermute(jnp.concatenate([left[:, 0:1024], right[:, 0:1024]] + extra,...  6.56 us
    ppermute x3, starting transfers between devices, on_device(): lax.ppermute(sends[m], AXES, family(m))  6.55 us
    all_to_all x1, starting transfers between devices, on_device(): lax.all_to_all(spread, AXES, split_axis=1, concat_axis=1, tiled=True, axi...  6.21 us
    ppermute x1, waiting for transfers between devices, on_device(): edge_down = lax.ppermute(total[:, :, 0:32].astype(BF), AXES, BAND_DOWN)  5.81 us
  transfers between devices with their start and end apart: 26, of which 7 were waited for; matrix products, arithmetic and copies ran while one was open for 10% of the time, Pallas kernels for 8%

profile of v2, /device:TPU:6, one launch (start us, length us, event | category | flops | bytes accessed | tf_op | source)
XLA Modules:
  0.0 213.1 jit_solution(12491813284152260773)
XLA Ops:
  0.6 1.2 convert_element_type.73
  2.6 0.8 pad_slice_fusion.2
  3.4 3.7 %collective-permute-start.3 = (bf16[8,72,32]{2,1,0:T(8,128)(2,1)}, bf16[8,72,32]{2,1,0:T(8,128)(2,1)}, u32[]{:S(2)}, u32[]{:S(2)}) collective-permute-start(bf16[8,72,32]{2,1,0:T(8,128)(2,1)} %get-tuple-element.79), channel_id=1, source_target_pairs={{0,1},{1,2},{2,3},{3,4},{4,5},{5,6},{6,7},{8,9},{9,10},{10,11},{11... | collective-permute-start | bytes 110600 | tf_op jit(solution)/shard_map/ppermute | solution.py:465
  7.1 2.1 collective-permute-start.4
  9.9 1.3 fusion.15
  11.1 2.3 %pack.1 = (bf16[80,1024]{1,0:T(8,128)(2,1)}, s32[1,512]{1,0:T(1,128)}) custom-call(f32[69,512]{1,0:T(8,128)} %values.1, f32[1,512]{1,0:T(1,128)} %bitcast.87, f32[2,512]{1,0:T(2,128)} %frac.1, s32[1,512]{1,0:T(1,128)} %bitcast.88, s32[1,512]{1,0:T(1,128)} %bitcast.89), custom_call_target="tpu_custom_call" | custom-call | tf_op jit(solution)/shard_map/pack/pallas_call | solution.py:486
  13.4 1.7 copy.29
  15.1 9.4 %all-to-all-start = ((bf16[80,32,32]{0,2,1:T(8,128)(2,1)}), bf16[80,32,32]{0,2,1:T(8,128)(2,1)}, u32[]{:S(2)}, u32[]{:S(2)}) async-start(bf16[80,32,32]{0,2,1:T(8,128)(2,1)} %bitcast.20), calls=%async_computation | async-start | bytes 524288 | tf_op jit(solution)/shard_map/all_to_all | solution.py:494
  24.5 0.7 copy.34
  25.4 1.3 slice_bitcast_fusion.2
  30.4 0.7 pad.41.cells
  31.2 1.3 stack.70.scal.refs_0_
  32.4 2.5 %split.1 = (bf16[8,72,128]{2,1,0:T(8,128)(2,1)}, bf16[8,72,128]{2,1,0:T(8,128)(2,1)}, bf16[8,72,128]{2,1,0:T(8,128)(2,1)}, bf16[8,72,128]{2,1,0:T(8,128)(2,1)}) custom-call(s32[24]{0:T(128)} %stack.70.scal.refs_0_, bf16[8,72,256]{2,1,0:T(8,128)(2,1)} %pad.41.cells, bf16[8,72,32]{2,1,0:T(8,128)(2,1)} %collective-permute-done.3.before, ...), custom_call_target="tpu_custom_call" | custom-call | tf_op jit(solution)/shard_map/split/pallas_call | solution.py:467
  34.9 3.6 %collective-permute-start.6 = (bf16[8,72,128]{2,1,0:T(8,128)(2,1)}, bf16[8,72,128]{2,1,0:T(8,128)(2,1)S(1)}, u32[]{:S(2)}, u32[]{:S(2)}) collective-permute-start(bf16[8,72,128]{2,1,0:T(8,128)(2,1)} %get-tuple-element.32), channel_id=1, source_target_pairs={{0,16},{8,24},{16,0},{24,8},{1,17},{9,25},{17,1},{25,9},{2,18},{10... | collective-permute-start | bytes 442376 | tf_op jit(solution)/shard_map/ppermute | solution.py:474
  38.6 2.9 %collective-permute-start.7 = (bf16[8,72,128]{2,1,0:T(8,128)(2,1)}, bf16[8,72,128]{2,1,0:T(8,128)(2,1)S(1)}, u32[]{:S(2)}, u32[]{:S(2)}) collective-permute-start(bf16[8,72,128]{2,1,0:T(8,128)(2,1)} %get-tuple-element.33), channel_id=1, source_target_pairs={{0,24},{8,0},{16,8},{24,16},{1,25},{9,1},{17,9},{25,17},{2,26},{10... | collective-permute-start | bytes 442376 | tf_op jit(solution)/shard_map/ppermute | solution.py:474
  41.5 1.1 copy.32.pay0
  43.1 5.5 %fusion.1 = (bf16[4,1536,256]{2,1,0:T(8,128)(2,1)}, bf16[4,1536,256]{2,1,0:T(8,128)(2,1)}) fusion(bf16[4,384,128]{2,1,0:T(8,128)(2,1)S(1)} %broadcast.46, bf16[4,384,128]{2,1,0:T(8,128)(2,1)} %get-tuple-element.66, bf16[4,384,128]{2,1,0:T(8,128)(2,1)S(1)} %get-tuple-element.65, bf16[4,384,128]{2,1,0:T(8,128)(2,1)S(1)} %get-tuple-element.64, ...), kind=kLoop, calls=%fused_computation.5 | loop fusion | flops 47185920 | bytes 9043968 | tf_op jit(solution)/shard_map/concatenate | solution.py:412
  49.3 2.1 order.1
  51.4 1.5 collective-permute-start.8
  52.9 1.8 collective-permute-start.9
  57.9 3.9 %compact.1 = (bf16[80,4096]{1,0:T(8,128)(2,1)}, f32[32,128]{1,0:T(8,128)}, s32[1]{0:T(128)}) custom-call(s32[24]{0:T(128)} %stack.70.scal.refs_0_, bf16[80,1024]{1,0:T(8,128)(2,1)} %copy-done.6, bf16[80,1024]{1,0:T(8,128)(2,1)} %copy-done.10, bf16[80,1024]{1,0:T(8,128)(2,1)} %copy-done.9, bf16[80,1024]{1,0:T(8,128)(2,1)} %copy-done.11), custom_call_target="tpu_custom_call" | custom-call | tf_op jit(solution)/shard_map/compact/pallas_call | solution.py:497
  62.7 37.4 %first_iteration.1 = (bf16[72,3200]{1,0:T(8,128)(2,1)}, bf16[72,3200]{1,0:T(8,128)(2,1)}) custom-call(s32[24]{0:T(128)} %stack.70.scal.refs_0_, s32[1]{0:T(128)} %get-tuple-element.29.refs_1_.count, bf16[16,72,128]{2,1,0:T(8,128)(2,1)} %copy-done.21, bf16[16,72,128]{2,1,0:T(8,128)(2,1)} %get-tuple-element.35.refs_3_, ...), custom_call_target="tpu_custom_call" | custom-call | flops 10000000000 | bytes 6000000 | tf_op jit(solution)/shard_map/first_iteration/pallas_call | solution.py:384
  100.1 2.6 %collective-permute-start.11 = (bf16[72,3200]{1,0:T(8,128)(2,1)}, bf16[72,3200]{1,0:T(8,128)(2,1)S(1)}, u32[]{:S(2)}, u32[]{:S(2)}) collective-permute-start(bf16[72,3200]{1,0:T(8,128)(2,1)} %get-tuple-element.37), channel_id=1, source_target_pairs={{32,0},{40,8},{48,16},{56,24},{57,25},{49,17},{41,9},{33,1},{34,2}... | collective-permute-start | bytes 1382408 | tf_op jit(solution)/shard_map/ppermute | solution.py:514
  102.6 10.2 %collective-permute-done.11 = bf16[72,3200]{1,0:T(8,128)(2,1)S(1)} collective-permute-done((bf16[72,3200]{1,0:T(8,128)(2,1)}, bf16[72,3200]{1,0:T(8,128)(2,1)S(1)}, u32[]{:S(2)}, u32[]{:S(2)}) %collective-permute-start.11) | collective-permute-done | bytes 460832 | tf_op jit(solution)/shard_map/ppermute | solution.py:514
  112.8 1.1 add_convert_fusion.refs_13_
  114.0 1.3 collective-permute-done.10
  115.3 1.1 add_convert_fusion.1.refs_12_
  116.5 3.0 %collective-permute-start.12 = (bf16[72,2304]{1,0:T(8,128)(2,1)S(1)}, bf16[72,2304]{1,0:T(8,128)(2,1)S(1)}, u32[]{:S(2)}, u32[]{:S(2)}) collective-permute-start(bf16[72,2304]{1,0:T(8,128)(2,1)S(1)} %get-tuple-element.81), channel_id=1, source_target_pairs={{0,8},{8,16},{16,24},{24,25},{25,17},{17,9},{9,1},{1,2},{2,10},{10... | collective-permute-start | bytes 995336 | tf_op jit(solution)/shard_map/ppermute | solution.py:519
  119.6 1.9 collective-permute-start.13
  121.5 2.7 %collective-permute-done.12.refs_14_ = bf16[72,2304]{1,0:T(8,128)(2,1)S(1)} collective-permute-done((bf16[72,2304]{1,0:T(8,128)(2,1)S(1)}, bf16[72,2304]{1,0:T(8,128)(2,1)S(1)}, u32[]{:S(2)}, u32[]{:S(2)}) %collective-permute-start.12) | collective-permute-done | bytes 331808 | tf_op jit(solution)/shard_map/ppermute | solution.py:519
  124.2 6.6 %collective-permute-done.13.refs_15_ = bf16[72,2304]{1,0:T(8,128)(2,1)S(1)} collective-permute-done((bf16[72,2304]{1,0:T(8,128)(2,1)S(1)}, bf16[72,2304]{1,0:T(8,128)(2,1)S(1)}, u32[]{:S(2)}, u32[]{:S(2)}) %collective-permute-start.13) | collective-permute-done | bytes 331808 | tf_op jit(solution)/shard_map/ppermute | solution.py:518
  131.5 39.5 %second_iteration.1 = (bf16[16,72,128]{2,1,0:T(8,128)(2,1)}, bf16[16,72,128]{2,1,0:T(8,128)(2,1)}, bf16[16,72,128]{2,1,0:T(8,128)(2,1)}, bf16[16,72,128]{2,1,0:T(8,128)(2,1)}, bf16[72,4096]{1,0:T(8,128)(2,1)}) custom-call(s32[24]{0:T(128)} %stack.70.scal.refs_0_, s32[1]{0:T(128)} %get-tuple-element.29.refs_1_.count, bf16[16,72,128]{2,1,0:T(8,128)(2,1)} %copy-done.21, ...), custom_call_target="tpu_custom_call" | custom-call | flops 10000000000 | bytes 6000000 | tf_op jit(solution)/shard_map/second_iteration/pallas_call | solution.py:384
  171.0 3.2 %collective-permute-start.15 = (bf16[16,72,128]{2,1,0:T(8,128)(2,1)}, bf16[16,72,128]{2,1,0:T(8,128)(2,1)S(1)}, u32[]{:S(2)}, u32[]{:S(2)}) collective-permute-start(bf16[16,72,128]{2,1,0:T(8,128)(2,1)} %get-tuple-element.42), channel_id=1, source_target_pairs={{32,0},{40,8},{48,16},{56,24},{57,25},{49,17},{41,9},{33,1},{34,2}... | collective-permute-start | bytes 884744 | tf_op jit(solution)/shard_map/ppermute | solution.py:523
  174.3 3.6 %expand.1 = (bf16[72,1024]{1,0:T(8,128)(2,1)}, bf16[72,1024]{1,0:T(8,128)(2,1)}, bf16[72,1024]{1,0:T(8,128)(2,1)}, bf16[72,1024]{1,0:T(8,128)(2,1)}) custom-call(s32[1]{0:T(128)} %get-tuple-element.29.refs_1_.count, f32[32,128]{1,0:T(8,128)} %get-tuple-element.47.posx, bf16[72,4096]{1,0:T(8,128)(2,1)} %get-tuple-element.48.found), custom_call_target="tpu_custom_call" | custom-call | tf_op jit(solution)/shard_map/expand/pallas_call | solution.py:525
  177.9 0.8 collective-permute-start.22
  178.7 2.5 %collective-permute-start.23 = (bf16[72,1024]{1,0:T(8,128)(2,1)}, bf16[72,1024]{1,0:T(8,128)(2,1)S(1)}, u32[]{:S(2)}, u32[]{:S(2)}) collective-permute-start(bf16[72,1024]{1,0:T(8,128)(2,1)} %get-tuple-element.52), channel_id=1, source_target_pairs={{0,24},{8,16},{16,8},{24,0},{1,25},{9,17},{17,9},{25,1},{2,26},{10... | collective-permute-start | bytes 442376 | tf_op jit(solution)/shard_map/ppermute | solution.py:533
  182.1 2.3 %gather.1 = (bf16[8,72,128]{2,1,0:T(8,128)(2,1)}, bf16[8,72,128]{2,1,0:T(8,128)(2,1)}, bf16[8,72,128]{2,1,0:T(8,128)(2,1)}, bf16[8,72,128]{2,1,0:T(8,128)(2,1)}) custom-call(s32[24]{0:T(128)} %stack.70.scal.refs_0_, bf16[16,72,128]{2,1,0:T(8,128)(2,1)} %get-tuple-element.39.low, bf16[16,72,128]{2,1,0:T(8,128)(2,1)} %copy-done.7, ...), custom_call_target="tpu_custom_call" | custom-call | tf_op jit(solution)/shard_map/gather/pallas_call | solution.py:540
  185.1 2.7 %collective-permute-start.17 = (bf16[8,72,128]{2,1,0:T(8,128)(2,1)}, bf16[8,72,128]{2,1,0:T(8,128)(2,1)S(1)}, u32[]{:S(2)}, u32[]{:S(2)}) collective-permute-start(bf16[8,72,128]{2,1,0:T(8,128)(2,1)} %get-tuple-element.45), channel_id=1, source_target_pairs={{16,0},{24,8},{0,16},{8,24},{17,1},{25,9},{1,17},{9,25},{18,2},{26... | collective-permute-start | bytes 442376 | tf_op jit(solution)/shard_map/ppermute | solution.py:547
  187.8 0.8 collective-permute-done.23
  188.7 1.0 add_convert_fusion.2
  189.6 0.8 copy.42
  190.5 6.2 %all-to-all-start.1 = ((bf16[72,32,32]{0,2,1:T(8,128)(2,1)}), bf16[72,32,32]{0,2,1:T(8,128)(2,1)S(1)}, u32[]{:S(2)}, u32[]{:S(2)}) async-start(bf16[72,32,32]{0,2,1:T(8,128)(2,1)} %bitcast.43), calls=%async_computation.1 | async-start | bytes 524288 | tf_op jit(solution)/shard_map/all_to_all | solution.py:536
  196.7 1.0 maximum_convert_fusion
  198.4 3.4 %collective-permute-start.19 = (bf16[8,72,32]{2,1,0:T(8,128)(2,1)S(1)}, bf16[8,72,32]{2,1,0:T(8,128)(2,1)S(1)}, u32[]{:S(2)}, u32[]{:S(2)}) collective-permute-start(bf16[8,72,32]{2,1,0:T(8,128)(2,1)S(1)} %get-tuple-element.74), channel_id=1, source_target_pairs={{0,1},{1,2},{2,3},{3,4},{4,5},{5,6},{6,7},{8,9},{9,10},{10,11},{11... | collective-permute-start | bytes 110600 | tf_op jit(solution)/shard_map/ppermute | solution.py:554
  201.8 2.5 %collective-permute-start.20 = (bf16[8,72,32]{2,1,0:T(8,128)(2,1)S(1)}, bf16[8,72,32]{2,1,0:T(8,128)(2,1)S(1)}, u32[]{:S(2)}, u32[]{:S(2)}) collective-permute-start(bf16[8,72,32]{2,1,0:T(8,128)(2,1)S(1)} %get-tuple-element.75), channel_id=1, source_target_pairs={{1,0},{2,1},{3,2},{4,3},{5,4},{6,5},{7,6},{9,8},{10,9},{11,10},{12... | collective-permute-start | bytes 110600 | tf_op jit(solution)/shard_map/ppermute | solution.py:555
  204.3 1.3 fusion.8
  206.1 5.8 %collective-permute-done.20 = bf16[8,72,32]{2,1,0:T(8,128)(2,1)S(1)} collective-permute-done((bf16[8,72,32]{2,1,0:T(8,128)(2,1)S(1)}, bf16[8,72,32]{2,1,0:T(8,128)(2,1)S(1)}, u32[]{:S(2)}, u32[]{:S(2)}) %collective-permute-start.20) | collective-permute-done | bytes 36896 | tf_op jit(solution)/shard_map/ppermute | solution.py:555
  212.1 1.0 copy.43
  (97 shorter events, 10.5 us)
Async XLA Ops:
  0.6 23.9 %copy-start = (bf16[4,9,128,128]{3,2,1,0:T(8,128)(2,1)S(1)}, bf16[4,9,128,128]{3,2,1,0:T(8,128)(2,1)}, u32[]{:S(2)}) copy-start(bf16[4,9,128,128]{3,2,1,0:T(8,128)(2,1)} %param.13) | copy-start | bytes 3538948
  1.9 0.7 copy-start.1
  3.4 29.0 %collective-permute-start.3 = (bf16[8,72,32]{2,1,0:T(8,128)(2,1)}, bf16[8,72,32]{2,1,0:T(8,128)(2,1)}, u32[]{:S(2)}, u32[]{:S(2)}) collective-permute-start(bf16[8,72,32]{2,1,0:T(8,128)(2,1)} %get-tuple-element.79), channel_id=1, source_target_pairs={{0,1},{1,2},{2,3},{3,4},{4,5},{5,6},{6,7},{8,9},{9,10},{10,11},{11... | collective-permute-start | bytes 110600 | tf_op jit(solution)/shard_map/ppermute | solution.py:465
  7.1 25.3 %collective-permute-start.4 = (bf16[8,72,32]{2,1,0:T(8,128)(2,1)}, bf16[8,72,32]{2,1,0:T(8,128)(2,1)}, u32[]{:S(2)}, u32[]{:S(2)}) collective-permute-start(bf16[8,72,32]{2,1,0:T(8,128)(2,1)} %get-tuple-element.78), channel_id=1, source_target_pairs={{1,0},{2,1},{3,2},{4,3},{5,4},{6,5},{7,6},{9,8},{10,9},{11,10},{12... | collective-permute-start | bytes 110600 | tf_op jit(solution)/shard_map/ppermute | solution.py:466
  15.1 26.4 %all-to-all-start = ((bf16[80,32,32]{0,2,1:T(8,128)(2,1)}), bf16[80,32,32]{0,2,1:T(8,128)(2,1)}, u32[]{:S(2)}, u32[]{:S(2)}) async-start(bf16[80,32,32]{0,2,1:T(8,128)(2,1)} %bitcast.20), calls=%async_computation | async-start | bytes 524288 | tf_op jit(solution)/shard_map/all_to_all | solution.py:494
  25.3 1.4 copy-start.18
  25.4 5.0 %copy-start.2 = (bf16[69,8,256]{2,0,1:T(8,128)(2,1)S(1)}, bf16[69,8,256]{2,0,1:T(8,128)(2,1)}, u32[]{:S(2)}) copy-start(bf16[69,8,256]{2,0,1:T(8,128)(2,1)} %copy-done.1) | copy-start | bytes 847876
  34.9 13.6 %collective-permute-start.5 = (bf16[8,72,128]{2,1,0:T(8,128)(2,1)}, bf16[8,72,128]{2,1,0:T(8,128)(2,1)S(1)}, u32[]{:S(2)}, u32[]{:S(2)}) collective-permute-start(bf16[8,72,128]{2,1,0:T(8,128)(2,1)} %get-tuple-element.31), channel_id=1, source_target_pairs={{0,8},{8,16},{16,24},{24,0},{1,9},{9,17},{17,25},{25,1},{2,10},{10... | collective-permute-start | bytes 442376 | tf_op jit(solution)/shard_map/ppermute | solution.py:474
  34.9 13.6 %collective-permute-start.6 = (bf16[8,72,128]{2,1,0:T(8,128)(2,1)}, bf16[8,72,128]{2,1,0:T(8,128)(2,1)S(1)}, u32[]{:S(2)}, u32[]{:S(2)}) collective-permute-start(bf16[8,72,128]{2,1,0:T(8,128)(2,1)} %get-tuple-element.32), channel_id=1, source_target_pairs={{0,16},{8,24},{16,0},{24,8},{1,17},{9,25},{17,1},{25,9},{2,18},{10... | collective-permute-start | bytes 442376 | tf_op jit(solution)/shard_map/ppermute | solution.py:474
  38.6 10.0 %collective-permute-start.7 = (bf16[8,72,128]{2,1,0:T(8,128)(2,1)}, bf16[8,72,128]{2,1,0:T(8,128)(2,1)S(1)}, u32[]{:S(2)}, u32[]{:S(2)}) collective-permute-start(bf16[8,72,128]{2,1,0:T(8,128)(2,1)} %get-tuple-element.33), channel_id=1, source_target_pairs={{0,24},{8,0},{16,8},{24,16},{1,25},{9,1},{17,9},{25,17},{2,26},{10... | collective-permute-start | bytes 442376 | tf_op jit(solution)/shard_map/ppermute | solution.py:474
  42.6 12.1 %copy-start.6 = (bf16[80,1024]{1,0:T(8,128)(2,1)}, bf16[80,1024]{1,0:T(8,128)(2,1)S(1)}, u32[]{:S(2)}) copy-start(bf16[80,1024]{1,0:T(8,128)(2,1)S(1)} %copy.32.pay0) | copy-start | bytes 491524
  42.6 12.2 %collective-permute-start.1 = (bf16[80,1024]{1,0:T(8,128)(2,1)S(1)}, bf16[80,1024]{1,0:T(8,128)(2,1)S(1)}, u32[]{:S(2)}, u32[]{:S(2)}) collective-permute-start(bf16[80,1024]{1,0:T(8,128)(2,1)S(1)} %copy.32.pay0), channel_id=1, source_target_pairs={{0,16},{8,24},{16,0},{24,8},{1,17},{9,25},{17,1},{25,9},{2,18},{10... | collective-permute-start | bytes 491528 | tf_op jit(solution)/shard_map/ppermute | solution.py:495
  43.0 11.6 %copy-start.16 = (bf16[69,128]{1,0:T(8,128)(2,1)S(1)}, bf16[69,128]{1,0:T(8,128)(2,1)}, u32[]{:S(2)}) copy-start(bf16[69,128]{1,0:T(8,128)(2,1)} %param.14) | copy-start | bytes 52996
  43.1 11.6 %copy-start.17 = (bf16[128,69]{0,1:T(8,128)(2,1)S(1)}, bf16[128,69]{0,1:T(8,128)(2,1)}, u32[]{:S(2)}) copy-start(bf16[128,69]{0,1:T(8,128)(2,1)} %param.12) | copy-start | bytes 52996
  48.6 0.7 copy-start.14
  48.6 0.7 copy-start.15
  51.4 10.4 %collective-permute-start.8 = (bf16[16,72,128]{2,1,0:T(8,128)(2,1)}, bf16[16,72,128]{2,1,0:T(8,128)(2,1)S(1)}, u32[]{:S(2)}, u32[]{:S(2)}) collective-permute-start(bf16[16,72,128]{2,1,0:T(8,128)(2,1)} %get-tuple-element.34.refs_4_), channel_id=1, source_target_pairs={{0,32},{8,40},{16,48},{24,56},{25,57},{17,49},{9,41},{1,33},{2,34}... | collective-permute-start | bytes 884744 | tf_op jit(solution)/shard_map/ppermute | solution.py:482
  52.9 9.0 %collective-permute-start.9 = (bf16[16,72,128]{2,1,0:T(8,128)(2,1)}, bf16[16,72,128]{2,1,0:T(8,128)(2,1)S(1)}, u32[]{:S(2)}, u32[]{:S(2)}) collective-permute-start(bf16[16,72,128]{2,1,0:T(8,128)(2,1)} %get-tuple-element.35.refs_3_), channel_id=1, source_target_pairs={{32,0},{40,8},{48,16},{56,24},{57,25},{49,17},{41,9},{33,1},{34,2}... | collective-permute-start | bytes 884744 | tf_op jit(solution)/shard_map/ppermute | solution.py:482
  54.7 1.9 collective-permute-start
  54.8 1.8 copy-start.9
  54.8 1.7 collective-permute-start.2
  57.2 0.7 copy-start.11
  61.8 0.7 copy-start.21
  61.9 0.8 copy-start.22
  100.1 12.8 %collective-permute-start.11 = (bf16[72,3200]{1,0:T(8,128)(2,1)}, bf16[72,3200]{1,0:T(8,128)(2,1)S(1)}, u32[]{:S(2)}, u32[]{:S(2)}) collective-permute-start(bf16[72,3200]{1,0:T(8,128)(2,1)} %get-tuple-element.37), channel_id=1, source_target_pairs={{32,0},{40,8},{48,16},{56,24},{57,25},{49,17},{41,9},{33,1},{34,2}... | collective-permute-start | bytes 1382408 | tf_op jit(solution)/shard_map/ppermute | solution.py:514
  102.6 12.7 %collective-permute-start.10 = (bf16[72,3200]{1,0:T(8,128)(2,1)}, bf16[72,3200]{1,0:T(8,128)(2,1)S(1)}, u32[]{:S(2)}, u32[]{:S(2)}) collective-permute-start(bf16[72,3200]{1,0:T(8,128)(2,1)} %get-tuple-element.38), channel_id=1, source_target_pairs={{0,32},{8,40},{16,48},{24,56},{25,57},{17,49},{9,41},{1,33},{2,34}... | collective-permute-start | bytes 1382408 | tf_op jit(solution)/shard_map/ppermute | solution.py:513
  114.0 16.8 %copy-start.4 = (bf16[72,3200]{1,0:T(8,128)(2,1)}, bf16[72,3200]{1,0:T(8,128)(2,1)S(1)}, u32[]{:S(2)}) copy-start(bf16[72,3200]{1,0:T(8,128)(2,1)S(1)} %add_convert_fusion.refs_13_) | copy-start | bytes 1382404
  116.4 14.4 %copy-start.5 = (bf16[72,3200]{1,0:T(8,128)(2,1)}, bf16[72,3200]{1,0:T(8,128)(2,1)S(1)}, u32[]{:S(2)}) copy-start(bf16[72,3200]{1,0:T(8,128)(2,1)S(1)} %add_convert_fusion.1.refs_12_) | copy-start | bytes 1382404
  116.5 7.7 %collective-permute-start.12 = (bf16[72,2304]{1,0:T(8,128)(2,1)S(1)}, bf16[72,2304]{1,0:T(8,128)(2,1)S(1)}, u32[]{:S(2)}, u32[]{:S(2)}) collective-permute-start(bf16[72,2304]{1,0:T(8,128)(2,1)S(1)} %get-tuple-element.81), channel_id=1, source_target_pairs={{0,8},{8,16},{16,24},{24,25},{25,17},{17,9},{9,1},{1,2},{2,10},{10... | collective-permute-start | bytes 995336 | tf_op jit(solution)/shard_map/ppermute | solution.py:519
  119.6 11.2 %collective-permute-start.13 = (bf16[72,2304]{1,0:T(8,128)(2,1)S(1)}, bf16[72,2304]{1,0:T(8,128)(2,1)S(1)}, u32[]{:S(2)}, u32[]{:S(2)}) collective-permute-start(bf16[72,2304]{1,0:T(8,128)(2,1)S(1)} %get-tuple-element.80), channel_id=1, source_target_pairs={{8,0},{16,8},{24,16},{25,24},{17,25},{9,17},{1,9},{2,1},{10,2},{18... | collective-permute-start | bytes 995336 | tf_op jit(solution)/shard_map/ppermute | solution.py:518
  124.2 6.6 %copy-start.19 = (bf16[72,2304]{1,0:T(8,128)(2,1)}, bf16[72,2304]{1,0:T(8,128)(2,1)S(1)}, u32[]{:S(2)}) copy-start(bf16[72,2304]{1,0:T(8,128)(2,1)S(1)} %collective-permute-done.12.refs_14_) | copy-start | bytes 995332
  130.8 0.7 copy-start.20
  171.0 10.3 %collective-permute-start.14 = (bf16[16,72,128]{2,1,0:T(8,128)(2,1)}, bf16[16,72,128]{2,1,0:T(8,128)(2,1)S(1)}, u32[]{:S(2)}, u32[]{:S(2)}) collective-permute-start(bf16[16,72,128]{2,1,0:T(8,128)(2,1)} %get-tuple-element.40), channel_id=1, source_target_pairs={{0,32},{8,40},{16,48},{24,56},{25,57},{17,49},{9,41},{1,33},{2,34}... | collective-permute-start | bytes 884744 | tf_op jit(solution)/shard_map/ppermute | solution.py:522
  171.0 10.3 %collective-permute-start.15 = (bf16[16,72,128]{2,1,0:T(8,128)(2,1)}, bf16[16,72,128]{2,1,0:T(8,128)(2,1)S(1)}, u32[]{:S(2)}, u32[]{:S(2)}) collective-permute-start(bf16[16,72,128]{2,1,0:T(8,128)(2,1)} %get-tuple-element.42), channel_id=1, source_target_pairs={{32,0},{40,8},{48,16},{56,24},{57,25},{49,17},{41,9},{33,1},{34,2}... | collective-permute-start | bytes 884744 | tf_op jit(solution)/shard_map/ppermute | solution.py:523
  177.9 9.9 %collective-permute-start.21 = (bf16[72,1024]{1,0:T(8,128)(2,1)}, bf16[72,1024]{1,0:T(8,128)(2,1)S(1)}, u32[]{:S(2)}, u32[]{:S(2)}) collective-permute-start(bf16[72,1024]{1,0:T(8,128)(2,1)} %get-tuple-element.50), channel_id=1, source_target_pairs={{0,8},{8,0},{16,24},{24,16},{1,9},{9,1},{17,25},{25,17},{2,10},{10... | collective-permute-start | bytes 442376 | tf_op jit(solution)/shard_map/ppermute | solution.py:533
  177.9 9.9 %collective-permute-start.22 = (bf16[72,1024]{1,0:T(8,128)(2,1)}, bf16[72,1024]{1,0:T(8,128)(2,1)S(1)}, u32[]{:S(2)}, u32[]{:S(2)}) collective-permute-start(bf16[72,1024]{1,0:T(8,128)(2,1)} %get-tuple-element.51), channel_id=1, source_target_pairs={{0,16},{8,24},{16,0},{24,8},{1,17},{9,25},{17,1},{25,9},{2,18},{10... | collective-permute-start | bytes 442376 | tf_op jit(solution)/shard_map/ppermute | solution.py:533
  178.7 9.9 %collective-permute-start.23 = (bf16[72,1024]{1,0:T(8,128)(2,1)}, bf16[72,1024]{1,0:T(8,128)(2,1)S(1)}, u32[]{:S(2)}, u32[]{:S(2)}) collective-permute-start(bf16[72,1024]{1,0:T(8,128)(2,1)} %get-tuple-element.52), channel_id=1, source_target_pairs={{0,24},{8,16},{16,8},{24,0},{1,25},{9,17},{17,9},{25,1},{2,26},{10... | collective-permute-start | bytes 442376 | tf_op jit(solution)/shard_map/ppermute | solution.py:533
  181.3 0.7 copy-start.7
  181.3 0.8 copy-start.8
  184.4 12.3 %collective-permute-start.16 = (bf16[8,72,128]{2,1,0:T(8,128)(2,1)}, bf16[8,72,128]{2,1,0:T(8,128)(2,1)S(1)}, u32[]{:S(2)}, u32[]{:S(2)}) collective-permute-start(bf16[8,72,128]{2,1,0:T(8,128)(2,1)} %get-tuple-element.44), channel_id=1, source_target_pairs={{8,0},{16,8},{24,16},{0,24},{9,1},{17,9},{25,17},{1,25},{10,2},{18... | collective-permute-start | bytes 442376 | tf_op jit(solution)/shard_map/ppermute | solution.py:547
  185.1 11.6 %collective-permute-start.17 = (bf16[8,72,128]{2,1,0:T(8,128)(2,1)}, bf16[8,72,128]{2,1,0:T(8,128)(2,1)S(1)}, u32[]{:S(2)}, u32[]{:S(2)}) collective-permute-start(bf16[8,72,128]{2,1,0:T(8,128)(2,1)} %get-tuple-element.45), channel_id=1, source_target_pairs={{16,0},{24,8},{0,16},{8,24},{17,1},{25,9},{1,17},{9,25},{18,2},{26... | collective-permute-start | bytes 442376 | tf_op jit(solution)/shard_map/ppermute | solution.py:547
  187.8 8.9 %collective-permute-start.18 = (bf16[8,72,128]{2,1,0:T(8,128)(2,1)}, bf16[8,72,128]{2,1,0:T(8,128)(2,1)S(1)}, u32[]{:S(2)}, u32[]{:S(2)}) collective-permute-start(bf16[8,72,128]{2,1,0:T(8,128)(2,1)} %get-tuple-element.46), channel_id=1, source_target_pairs={{24,0},{0,8},{8,16},{16,24},{25,1},{1,9},{9,17},{17,25},{26,2},{2,... | collective-permute-start | bytes 442376 | tf_op jit(solution)/shard_map/ppermute | solution.py:547
  190.5 13.8 %all-to-all-start.1 = ((bf16[72,32,32]{0,2,1:T(8,128)(2,1)}), bf16[72,32,32]{0,2,1:T(8,128)(2,1)S(1)}, u32[]{:S(2)}, u32[]{:S(2)}) async-start(bf16[72,32,32]{0,2,1:T(8,128)(2,1)} %bitcast.43), calls=%async_computation.1 | async-start | bytes 524288 | tf_op jit(solution)/shard_map/all_to_all | solution.py:536
  197.8 6.5 %copy-start.12 = (f32[69,512]{1,0:T(8,128)S(1)}, f32[69,512]{1,0:T(8,128)}, u32[]{:S(2)}) copy-start(f32[69,512]{1,0:T(8,128)} %values.1) | copy-start | bytes 423940
  197.8 6.5 %copy-start.23 = (s32[1,512]{1,0:T(1,128)S(1)}, s32[1,512]{1,0:T(1,128)}, u32[]{:S(2)}) copy-start(s32[1,512]{1,0:T(1,128)} %get-tuple-element.53) | copy-start | bytes 6148
  197.9 14.0 %copy-start.3 = (f32[69,8,256]{2,1,0:T(8,128)S(1)}, f32[69,8,256]{2,1,0:T(8,128)}, u32[]{:S(2)}) copy-start(f32[69,8,256]{2,1,0:T(8,128)} %param.11) | copy-start | bytes 1695748
  198.4 7.7 %collective-permute-start.19 = (bf16[8,72,32]{2,1,0:T(8,128)(2,1)S(1)}, bf16[8,72,32]{2,1,0:T(8,128)(2,1)S(1)}, u32[]{:S(2)}, u32[]{:S(2)}) collective-permute-start(bf16[8,72,32]{2,1,0:T(8,128)(2,1)S(1)} %get-tuple-element.74), channel_id=1, source_target_pairs={{0,1},{1,2},{2,3},{3,4},{4,5},{5,6},{6,7},{8,9},{9,10},{10,11},{11... | collective-permute-start | bytes 110600 | tf_op jit(solution)/shard_map/ppermute | solution.py:554
  201.8 10.1 %collective-permute-start.20 = (bf16[8,72,32]{2,1,0:T(8,128)(2,1)S(1)}, bf16[8,72,32]{2,1,0:T(8,128)(2,1)S(1)}, u32[]{:S(2)}, u32[]{:S(2)}) collective-permute-start(bf16[8,72,32]{2,1,0:T(8,128)(2,1)S(1)} %get-tuple-element.75), channel_id=1, source_target_pairs={{1,0},{2,1},{3,2},{4,3},{5,4},{6,5},{7,6},{9,8},{10,9},{11,10},{12... | collective-permute-start | bytes 110600 | tf_op jit(solution)/shard_map/ppermute | solution.py:555
  (2 other events, 1.3 us)
